TPU v7x, 512 devices: a whole 4x8x8 slice. The times are simulated.
512 devices in a mesh: lon: 64 (over z, y_hi, core), ch: 8 (over x, y_lo).
Axes of the slice: x: 4, y: 8 (y_hi: 4, y_lo: 2; y = y_hi * 2 + y_lo), z: 8, core: 2. Of those that a mesh axis runs over, the one named last changes fastest.
Arguments:
- features: bfloat16 [512, 1, 8, 8192], P('ch', None, None, 'lon'), may hold values from -160 to 160, as said below
- group_norm_gain: float32 [512], P('ch'), may hold values from 0.5 to 2
- group_norm_bias: float32 [512], P('ch'), may hold values from -1 to 1
- kernel: bfloat16 [3, 3, 512, 512], P(None, None, 'ch'), may hold values from -0.058925565 to 0.058925565, as said below
- cotangent: bfloat16 [512, 1, 8, 8192], P('ch', None, None, 'lon'), may hold values from -10 to 10, as said below
Outputs:
- conv_out: bfloat16 [512, 1, 8, 8192], P('ch', None, None, 'lon')
- feature_map_gradient: bfloat16 [512, 1, 8, 8192], P('ch', None, None, 'lon')
- kernel_grad: float32 [3, 3, 512, 512], P(None, None, 'ch')
Inputs may be any that keep to these rules, and one draw needn't show every extreme that they name: `features`: Real-valued feature map whose magnitude varies between rows and between longitudes, with a per-channel offset. `kernel`: Real-valued weights of standard deviation about (4608)^(-1/2). `cotangent`: Real-valued output gradient.
All inputs are finite; a program needn't handle non-finite values.
Results may differ from a plain program's by a relative error of at most 0.005.
Values may be sent and summed in bfloat16 or wider, within the bound.
A program may use at most 64 MiB of HBM per device.

v0:
```python
import jax
import jax.numpy as jnp
from jax import lax
from jax.sharding import PartitionSpec as P

C = 512
G = 32


def extended(block, sides, width):
    for axis, dim in sides:
        count = lax.axis_size(axis)
        forward = [(i, i + 1) for i in range(count - 1)]
        forward.append((count - 1, 0))
        backward = [(target, source) for source, target in forward]
        low = lax.ppermute(
            lax.slice_in_dim(block, block.shape[dim] - width, None, axis=dim), axis, forward
        )
        high = lax.ppermute(lax.slice_in_dim(block, 0, width, axis=dim), axis, backward)
        block = jnp.concatenate([low, block, high], axis=dim)
    return block


def pad_rows(field):
    return jnp.pad(field, ((0, 0), (0, 0), (1, 1), (0, 0)))


def strip_groups(field, channels_per_group):
    return field.reshape(field.shape[0] // channels_per_group, -1).sum(axis=1)


def group_variance(values, channels_per_group):
    return jnp.repeat(values, channels_per_group)[:, None, None, None]


def per_device(features, group_norm_gain, group_norm_bias, kernel, cotangent):
    channels_per_group = C // G
    chans, frames, height, width = features.shape
    out_local = cotangent.shape[0]
    strips = lax.axis_size("lon")
    element_count = float(channels_per_group * frames * height * width * strips)
    feature_map = features.astype(jnp.float32)
    first_moment, second_moment = lax.psum(
        (
            strip_groups(feature_map, channels_per_group),
            strip_groups(feature_map * feature_map, channels_per_group),
        ),
        "lon",
    )
    group_mean = first_moment / element_count
    var = second_moment / element_count - group_mean * group_mean
    inverse_deviation = 1.0 / jnp.sqrt(var + 1e-06)
    normalized_input = (
        feature_map - group_variance(group_mean, channels_per_group)
    ) * group_variance(inverse_deviation, channels_per_group)
    preactivation = (
        normalized_input * group_norm_gain[:, None, None, None]
        + group_norm_bias[:, None, None, None]
    )
    sig = jax.nn.sigmoid(preactivation)
    act = (preactivation * sig).astype(jnp.bfloat16)
    act_rim = extended(act, (("lon", 3),), 1)
    act_pad = pad_rows(act_rim)
    sliced = kernel
    total = jnp.zeros((lax.axis_size("ch") * out_local, frames, height, width), jnp.float32)
    for row_off in range(3):
        for col_off in range(3):
            patch = act_pad[:, :, row_off : row_off + height, col_off : col_off + width]
            total = total + jnp.einsum(
                "co,cfhw->ofhw", sliced[row_off, col_off], patch, preferred_element_type=jnp.float32
            )
    conv_out = lax.psum_scatter(total, "ch", scatter_dimension=0, tiled=True)
    grad_rim = extended(cotangent, (("lon", 3),), 1)
    piece = lax.all_gather(grad_rim, "ch", axis=0, tiled=True)
    act_grad = jnp.zeros((chans, frames, height, width), jnp.float32)
    padded = pad_rows(piece)
    interior = piece[:, :, :, 1 : 1 + width]
    sliced = kernel
    grad_rows = []
    for row_off in range(3):
        grad_cols = []
        for col_off in range(3):
            back = padded[
                :, :, 2 - row_off : 2 - row_off + height, 2 - col_off : 2 - col_off + width
            ]
            act_grad = act_grad + jnp.einsum(
                "co,ofhw->cfhw", sliced[row_off, col_off], back, preferred_element_type=jnp.float32
            )
            patch = act_pad[:, :, row_off : row_off + height, col_off : col_off + width]
            grad_cols.append(
                jnp.einsum("cfhw,ofhw->co", patch, interior, preferred_element_type=jnp.float32)
            )
        grad_rows.append(jnp.stack(grad_cols))
    block = jnp.stack(grad_rows)
    act_grad, kern_local = (act_grad, block)
    kernel_grad = lax.psum(kern_local, "lon") * float(frames * height * width * strips) ** (-0.5)
    preactivation_gradient = act_grad * sig * (1.0 + preactivation * (1.0 - sig))
    normalized_input_gradient = preactivation_gradient * group_norm_gain[:, None, None, None]
    linear_sum, quadratic_sum = lax.psum(
        (
            strip_groups(normalized_input_gradient, channels_per_group),
            strip_groups(normalized_input_gradient * normalized_input, channels_per_group),
        ),
        "lon",
    )
    feature_map_gradient = group_variance(inverse_deviation, channels_per_group) * (
        normalized_input_gradient
        - group_variance(linear_sum, channels_per_group) / element_count
        - normalized_input * group_variance(quadratic_sum, channels_per_group) / element_count
    )
    return (conv_out.astype(jnp.bfloat16), feature_map_gradient.astype(jnp.bfloat16), kernel_grad)


def solution(mesh):
    in_specs = (
        P("ch", None, None, "lon"),
        P("ch"),
        P("ch"),
        P(None, None, "ch", None),
        P("ch", None, None, "lon"),
    )
    out_specs = (P("ch", None, None, "lon"), P("ch", None, None, "lon"), P(None, None, "ch", None))
    return jax.shard_map(
        per_device, mesh=mesh, in_specs=in_specs, out_specs=out_specs, check_vma=False
    )
```

profile of v0, /device:TPU:1, one launch (start us, length us, event | category | flops | bytes accessed | tf_op | source)
XLA Modules:
  0.0 954.2 jit_solution(948961613600961186)
XLA Ops:
  7.2 1.0 copy.16
  8.2 0.1 fusion.105
  8.3 5.6 collective-permute-start.2
  13.9 5.1 collective-permute-start.3
  19.1 3.5 collective-permute-done.3
  22.5 0.9 pad_maximum_fusion.1
  23.5 1.0 convert_reduce_fusion
  24.5 0.1 reduce_sum.47
  24.6 0.1 reduce_sum.53
  24.7 0.1 reduce_sum.51
  24.8 0.1 reduce_sum.54
  24.9 145.9 %all-reduce.3 = (f32[4]{0:T(128)S(1)}, f32[4]{0:T(128)S(1)}) all-reduce(f32[4]{0:T(128)S(1)} %reduce_sum.54, f32[4]{0:T(128)S(1)} %reduce_sum.51), channel_id=1, replica_groups=mesh['lon'=64,'ch'=8] {'lon'}, use_global_device_ids=true, to_apply=%region_5.6 | all-reduce | flops 8 | bytes 64 | tf_op jit(solution)/shard_map/psum | solution.py:43
  170.9 0.1 sub.27
  171.1 0.1 mul.69
  171.2 2.2 fusion.15
  173.4 0.5 convolution_add_fusion.7
  174.0 0.3 convolution_add_fusion.6
  174.3 0.5 convolution_add_fusion.5
  174.8 0.6 convolution_add_fusion.4
  175.4 0.3 convolution_add_fusion.3
  175.7 0.6 convolution_add_fusion.2
  176.3 0.6 convolution_add_fusion.1
  176.9 0.4 fusion.104
  177.3 0.1 reduce_sum.59
  177.4 0.1 reduce_sum.72
  177.5 0.1 reduce_sum.74
  177.6 0.1 reduce_sum.75
  177.7 144.3 %all-reduce.2 = (f32[4]{0:T(128)S(1)}, f32[4]{0:T(128)S(1)}) all-reduce(f32[4]{0:T(128)S(1)} %reduce_sum.75, f32[4]{0:T(128)S(1)} %reduce_sum.72), channel_id=1, replica_groups=mesh['lon'=64,'ch'=8] {'lon'}, use_global_device_ids=true, to_apply=%region_12.13 | all-reduce | flops 8 | bytes 64 | tf_op jit(solution)/shard_map/psum | solution.py:99
  322.1 0.1 div.26
  322.3 0.1 mul.80
  322.4 0.3 fusion.40
  322.6 0.1 fusion.106
  322.7 1.8 fusion.45
  324.5 1.9 collective-permute-start
  326.4 2.6 collective-permute-start.1
  329.0 0.5 convolution_bitcast_fusion.4
  329.6 4.7 collective-permute-done.1
  334.2 0.2 fusion.22
  334.4 1.9 fusion.51
  336.3 1.9 fusion.50
  338.2 1.9 fusion.49
  340.0 1.9 fusion.48
  341.9 1.8 fusion.47
  343.7 0.6 convolution_bitcast_fusion
  344.3 0.6 convolution_bitcast_fusion.1
  344.9 0.5 convolution_bitcast_fusion.2
  345.4 0.6 convolution_bitcast_fusion.5
  346.1 0.6 convolution_bitcast_fusion.3
  346.7 0.6 convolution_bitcast_fusion.6
  347.3 0.6 convolution_bitcast_fusion.7
  347.9 0.5 convolution_bitcast_fusion.8
  348.4 0.1 maximum_bitcast_fusion
  348.5 1.1 pad_maximum_fusion
  349.7 0.5 fusion.64
  350.3 0.5 fusion.52
  350.8 0.4 copy-done.1
  351.2 0.6 copy-done.2
  351.9 6.2 add_bitcast_fusion
  358.1 3.0 copy.15
  361.1 0.7 copy.19
  361.8 526.2 %all-reduce.6.cloned.1.call-done = f32[3,3,64,512]{3,2,1,0:T(8,128)} async-done(((f32[3,3,64,512]{3,2,1,0:T(8,128)}), f32[3,3,64,512]{3,2,1,0:T(8,128)}) %all-reduce.6.cloned.1.call-update) | async-done | bytes 1179664 | tf_op jit(solution)/shard_map/psum | solution.py:96
  888.1 2.4 broadcast_multiply_fusion
  890.5 55.5 %reduce-scatter.2.cloned.1.call-done = f32[64,1,8,128]{3,2,1,0:T(8,128)} async-done(((f32[512,1,8,128]{3,2,1,0:T(8,128)}), f32[64,1,8,128]{3,2,1,0:T(8,128)}) %reduce-scatter.2.cloned.1.call-update) | async-done | bytes 262160 | tf_op jit(solution)/shard_map/reduce_scatter | solution.py:72
  946.0 1.6 convert_element_type.18
  (28 shorter events, 0.5 us)
Async XLA Ops:
  7.2 166.3 %copy-start.3 = (bf16[3,3,64,512]{3,2,1,0:T(8,128)(2,1)S(1)}, bf16[3,3,64,512]{3,2,1,0:T(8,128)(2,1)}, u32[]{:S(2)}) copy-start(bf16[3,3,64,512]{3,2,1,0:T(8,128)(2,1)} %param.8) | copy-start | bytes 1769476
  7.2 164.0 %all-gather.2.cloned.1.call-start = ((), (), s32[]{:S(2)}) async-start(), calls=%async_computation.2 | async-start | bytes 2359296 | tf_op jit(solution)/shard_map/all_gather | solution.py:74
  8.3 10.7 %collective-permute-start.2 = (bf16[64,1,8,1]{3,0,2,1:T(8,128)(2,1)S(1)}, bf16[64,1,8,1]{3,0,2,1:T(8,128)(2,1)S(1)}, u32[]{:S(2)}, u32[]{:S(2)}) collective-permute-start(bf16[64,1,8,1]{3,0,2,1:T(8,128)(2,1)S(1)} %get-tuple-element.19), channel_id=1, source_target_pairs={{0,8},{8,16},{16,24},{24,32},{32,40},{40,48},{48,56},{56,64},{64,7... | collective-permute-start | bytes 3080 | tf_op jit(solution)/shard_map/ppermute | solution.py:16
  13.9 8.6 collective-permute-start.3
  23.4 864.7 %all-reduce.6.cloned.1.call-start = ((), (), s32[]{:S(2)}) async-start(), calls=%async_computation.3 | async-start | bytes 2359296 | tf_op jit(solution)/shard_map/psum | solution.py:96
  171.2 2.3 copy-start
  175.7 1.2 copy-start.4
  175.7 1.1 copy-start.5
  175.7 1.1 copy-start.6
  324.5 5.0 collective-permute-start
  326.4 7.8 collective-permute-start.1
  349.6 1.6 copy-start.1
  349.7 596.4 %reduce-scatter.2.cloned.1.call-start = ((), (), s32[]{:S(2)}) async-start(), calls=%async_computation.1 | async-start | bytes 2359296 | tf_op jit(solution)/shard_map/reduce_scatter | solution.py:72
  349.7 2.2 copy-start.2
Sparse Core Ops, SparseCore 0:
  23.5 61.3 all-gather.1
  349.8 538.2 all-reduce.5
  891.2 54.8 reduce-scatter.1
where the time goes:
time: 955 us; the launch traced here: 954 us
  waiting for transfers between devices  590 us (62%)
  blocking collectives  290 us (30%)
  matrix products  29.6 us (3%)
  starting transfers between devices  15.3 us (2%)
  between operations  14 us (1%)
    psum x1, waiting for transfers between devices, per_device(): lax.psum(kern_local, 'lon')  526 us
    psum x1, blocking collectives, per_device(): lax.psum((strip_groups(feature_map, channels_per_group), strip_groups(fea...  146 us
    psum x1, blocking collectives, per_device(): lax.psum((strip_groups(normalized_input_gradient, channels_per_group), st...  144 us
    reduce_scatter x1, waiting for transfers between devices, per_device(): conv_out = lax.psum_scatter(total, 'ch', scatter_dimension=0, tiled=True)  55.5 us
  transfers between devices with their start and end apart: 7, of which 4 were waited for; matrix products, arithmetic and copies ran while one was open for 2% of the time, Pallas kernels for 0%

commit v1 on v0

v1 whole, which is shorter than its diff:
```python
import functools

import jax
import jax.numpy as jnp
from jax import lax
from jax.experimental import pallas as pl
from jax.experimental.pallas import tpu as pltpu
from jax.sharding import PartitionSpec as P

C = 512
G = 32
CL = 64
H = 8
W = 128
S = H * W
NZ, NY = 8, 4
OWN_Z = 6
NQ = OWN_Z * NY
CH = 48
MESH = pl.DeviceIdType.MESH
F32 = jnp.float32
BF16 = jnp.bfloat16


def body(
    feat, gain, bias, w, cot,
    conv_out, fgrad, kgrad,
    tmp, x2, xh, dact, patch, wt, cotall, halo, edge, edge_in,
    y_st, z_st, y_t, z_t, convb, convr, g3, gsend, gcore, hb, rsbuf, gfin, zz, agr,
    edge_s, edge_r, cot_s, cot_r, halo_s, halo_r,
    yst_s, yst_r, zst_s, zst_r, yt_s, yt_r, zt_s, zt_r,
    conv_s, conv_r, core_s, core_r, rs_s, rs_r, ag_s, ag_r, fw_s, fw_r,
):
    lon = lax.axis_index("lon")
    ch = lax.axis_index("ch")
    z, yc = lon // 8, lon % 8
    yh, core = yc // 2, yc % 2
    n_lon = 64

    def at_lon(d):
        return (lax.rem(lon + d + n_lon, n_lon), ch)

    def at_ch(k):
        return (lon, lax.rem(ch + k, 8))

    def at_yc(k):
        return (z * 8 + lax.rem(yc + k, 8), ch)

    def at_z(k):
        return (lax.rem(z + k, 8) * 8 + yc, ch)

    partner = (lon + 1 - 2 * core, ch)

    def remote(src, dst, ss, rs, dev):
        return pltpu.make_async_remote_copy(
            src_ref=src, dst_ref=dst, send_sem=ss, recv_sem=rs, device_id=dev, device_id_type=MESH
        )

    barrier = pltpu.get_barrier_semaphore()
    for k in range(1, 8):
        for where in (at_ch, at_yc, at_z):
            pl.semaphore_signal(barrier, inc=1, device_id=where(k), device_id_type=MESH)
    for d in (-1, 1):
        pl.semaphore_signal(barrier, inc=1, device_id=at_lon(d), device_id_type=MESH)

    lane = lax.broadcasted_iota(jnp.int32, (CL, W), 1)
    group = lax.broadcasted_iota(jnp.int32, (CL, W), 0) // 16

    my_rows = pl.ds(pl.multiple_of(ch * CL, CL), CL)

    tmp[...] = cot[...].astype(F32)
    e = jnp.zeros((CL, W), F32)
    for h in range(H):
        row = tmp[pl.ds(h, CL, stride=H), :]
        cotall[my_rows, h * W:(h + 1) * W] = row.astype(BF16)
        e = jnp.where(lane == h, row[:, W - 1:W], e)
        e = jnp.where(lane == H + h, row[:, 0:1], e)
    edge[0:CL, :] = e.astype(BF16)
    tmp[...] = feat[...].astype(F32)
    e = jnp.zeros((CL, W), F32)
    total = jnp.zeros((CL, W), F32)
    total2 = jnp.zeros((CL, W), F32)
    for h in range(H):
        row = tmp[pl.ds(h, CL, stride=H), :]
        x2[:, h * W:(h + 1) * W] = row
        total += row
        total2 += row * row
        e = jnp.where(lane == h, row[:, W - 1:W], e)
        e = jnp.where(lane == H + h, row[:, 0:1], e)
    edge[CL:2 * CL, :] = e.astype(BF16)

    def pack(a, b):
        a = jnp.sum(a, axis=1, keepdims=True)
        b = jnp.sum(b, axis=1, keepdims=True)
        both = jnp.where(lane == group, a, 0.0) + jnp.where(lane == group + 4, b, 0.0)
        return jnp.sum(both, axis=0, keepdims=True)

    def unpack(vec):
        full = jnp.broadcast_to(vec, (CL, W))
        a = jnp.sum(jnp.where(lane == group, full, 0.0), axis=1, keepdims=True)
        b = jnp.sum(jnp.where(lane == group + 4, full, 0.0), axis=1, keepdims=True)
        return a, b

    def column(ref):
        r = lax.broadcasted_iota(jnp.int32, (CL, CL), 0)
        c = lax.broadcasted_iota(jnp.int32, (CL, CL), 1)
        return jnp.sum(jnp.where(r == c, jnp.broadcast_to(ref[...], (CL, CL)), 0.0), axis=1, keepdims=True)

    def peers_copy(buf, ss, rs, where):
        return [remote(buf.at[0], buf.at[k], ss.at[k], rs.at[k], where(k)) for k in range(1, 8)]

    def add_up(buf):
        acc = buf[0]
        for k in range(1, 8):
            acc = acc + buf[k]
        return acc

    y_st[0] = pack(total, total2)
    pl.semaphore_wait(barrier, 23)

    yst = peers_copy(y_st, yst_s, yst_r, at_yc)
    for cp in yst:
        cp.start()
    edges = [
        remote(edge, edge_in.at[0], edge_s.at[0], edge_r.at[0], at_lon(1)),
        remote(edge, edge_in.at[1], edge_s.at[1], edge_r.at[1], at_lon(-1)),
    ]
    for cp in edges:
        cp.start()
    cots = [
        remote(cotall.at[my_rows], cotall.at[my_rows], cot_s.at[k], cot_r.at[k], at_ch(k))
        for k in (4, 3, 5, 2, 6, 7, 1)
    ]
    for cp in cots:
        cp.start()

    for i in range(4):
        wt[:, i * 128:(i + 1) * 128] = w[i * 128:(i + 1) * 128, :].astype(F32).T.astype(BF16)
    wt[:, 512:576] = w[512:576, :].astype(F32).T.astype(BF16)

    for cp in yst:
        cp.wait_recv()
    z_st[0] = add_up(y_st)
    zst = peers_copy(z_st, zst_s, zst_r, at_z)
    for cp in zst:
        cp.start()

    for cp in edges:
        cp.wait_recv()
    lane2 = lax.broadcasted_iota(jnp.int32, (2 * CL, W), 1)
    rim = jnp.where(lane2 < H, edge_in[0].astype(F32), edge_in[1].astype(F32))
    halo[my_rows, :] = rim[0:CL].astype(BF16)
    halos = [
        remote(halo.at[my_rows], halo.at[my_rows], halo_s.at[k], halo_r.at[k], at_ch(k))
        for k in range(1, 8)
    ]
    for cp in halos:
        cp.start()

    gain_c = column(gain)
    bias_c = column(bias)
    n = float(16 * H * W * n_lon)
    zero = jnp.zeros((192, W), BF16)
    patch[0:192, 0:W] = zero
    patch[384:576, S - W:S] = zero

    for cp in zst:
        cp.wait_recv()
    m1, m2 = unpack(add_up(z_st))
    mean = m1 / n
    var = m2 / n - mean * mean
    rstd = 1.0 / jnp.sqrt(var + 1e-06)

    rim_pre = (rim[CL:2 * CL] - mean) * rstd * gain_c + bias_c
    rim_act = rim_pre * jax.nn.sigmoid(rim_pre)
    for h in range(H):
        cols = slice(h * W, (h + 1) * W)
        norm = (x2[:, cols] - mean) * rstd
        pre = norm * gain_c + bias_c
        sig = jax.nn.sigmoid(pre)
        xh[:, cols] = norm
        dact[:, cols] = sig * (1.0 + pre * (1.0 - sig)) * gain_c
        act = pre * sig
        left = jnp.where(lane == 0, rim_act[:, h:h + 1], pltpu.roll(act, 1, 1))
        right = jnp.where(lane == W - 1, rim_act[:, H + h:H + h + 1], pltpu.roll(act, W - 1, 1))
        for s, v in enumerate((left, act, right)):
            v = v.astype(BF16)
            for r in range(3):
                to = h + 1 - r
                if 0 <= to < H:
                    patch[r * 192 + s * CL:r * 192 + (s + 1) * CL, to * W:(to + 1) * W] = v

    for cp in cots:
        cp.wait_recv()

    def kg_step(i, _):
        rows = pl.ds(pl.multiple_of(i * 256, 256), 256)
        part = lax.dot_general(
            patch[...], cotall[rows, :], (((1,), (1,)), ((), ())), preferred_element_type=F32
        )
        for rc in range(12):
            for c in range(2):
                g3[rc // 6, (rc % 6) * 4 + 2 * i + c] = part[rc * CH:(rc + 1) * CH, c * W:(c + 1) * W]
        return 0

    lax.fori_loop(0, 2, kg_step, 0)
    gsend[...] = g3[1 - core].astype(BF16)
    swap = remote(gsend, gcore, core_s.at[0], core_r.at[0], partner)
    swap.start()

    def conv_step(i, _):
        cols = pl.ds(pl.multiple_of(i * 256, 256), 256)
        convb[:, cols] = jnp.dot(wt[...], patch[:, cols], preferred_element_type=F32).astype(BF16)
        return 0

    swap.wait_recv()
    hb[...] = (g3[core] + gcore[...].astype(F32)).astype(BF16)

    def target(k):
        tz, ty = lax.rem(z + k // NY, NZ), lax.rem(yh + k % NY, NY)
        return tz, ty, (tz * 8 + ty * 2 + core, ch)

    my_q = z * NY + yh
    owner = z < OWN_Z

    def rs_copy(k):
        tz, ty, dev = target(k)
        return tz, remote(hb.at[lax.min(tz, OWN_Z - 1) * NY + ty], rsbuf.at[k], rs_s.at[k], rs_r.at[k], dev)

    def rs_send(k, _):
        tz, cp = rs_copy(k)

        @pl.when(tz < OWN_Z)
        def _():
            cp.start()

        return 0

    lax.fori_loop(1, 32, rs_send, 0)

    lax.fori_loop(0, 4, conv_step, 0)

    def ch_rows(k):
        return pl.ds(pl.multiple_of(lax.rem(ch + k, 8) * CL, CL), CL)

    convs = [
        remote(convb.at[ch_rows(k)], convr.at[k], conv_s.at[k], conv_r.at[k], at_ch(k))
        for k in (4, 3, 5, 2, 6, 7, 1)
    ]
    for cp in convs:
        cp.start()

    for cp in halos:
        cp.wait_recv()

    def z_step(i, _):
        cols = pl.ds(pl.multiple_of(i * 256, 256), 256)
        zz[:, cols] = jnp.dot(w[...], cotall[:, cols], preferred_element_type=F32)
        return 0

    lax.fori_loop(0, 4, z_step, 0)
    zh = jnp.dot(w[...], halo[...], preferred_element_type=F32)

    def zrows(r, s):
        return slice(r * 192 + s * CL, r * 192 + (s + 1) * CL)

    def rim_sum(s):
        up = jnp.where((lane % H) < H - 1, pltpu.roll(zh[zrows(0, s)], W - 1, 1), 0.0)
        down = jnp.where((lane % H) > 0, pltpu.roll(zh[zrows(2, s)], 1, 1), 0.0)
        return up + zh[zrows(1, s)] + down

    rim0, rim2 = rim_sum(0), rim_sum(2)
    t1 = jnp.zeros((CL, W), F32)
    t2 = jnp.zeros((CL, W), F32)
    for h in range(H):
        u = []
        for s in range(3):
            acc = zz[zrows(1, s), h * W:(h + 1) * W]
            if h + 1 < H:
                acc = acc + zz[zrows(0, s), (h + 1) * W:(h + 2) * W]
            if h >= 1:
                acc = acc + zz[zrows(2, s), (h - 1) * W:h * W]
            u.append(acc)
        agrad = u[1]
        agrad = agrad + jnp.where(lane == W - 1, rim0[:, H + h:H + h + 1], pltpu.roll(u[0], W - 1, 1))
        agrad = agrad + jnp.where(lane == 0, rim2[:, h:h + 1], pltpu.roll(u[2], 1, 1))
        cols = slice(h * W, (h + 1) * W)
        ng = agrad * dact[:, cols]
        agr[:, cols] = ng
        t1 += ng
        t2 += ng * xh[:, cols]
    y_t[0] = pack(t1, t2)
    yt = peers_copy(y_t, yt_s, yt_r, at_yc)
    for cp in yt:
        cp.start()

    def ag_copy(k):
        _, _, dev = target(k)
        q = lax.min(z, OWN_Z - 1) * NY + yh
        return remote(gfin.at[core, q], gfin.at[core, q], ag_s.at[k], ag_r.at[q], dev)

    @pl.when(owner)
    def _():
        def take(k, acc):
            rs_copy(k)[1].wait_recv()
            return acc + rsbuf[k].astype(F32)

        acc = lax.fori_loop(1, 32, take, hb[my_q].astype(F32))
        gfin[core, my_q] = acc.astype(BF16)

        def give(k, _):
            ag_copy(k).start()
            return 0

        lax.fori_loop(1, 32, give, 0)

    for cp in yt:
        cp.wait_recv()
    z_t[0] = add_up(y_t)
    zt = peers_copy(z_t, zt_s, zt_r, at_z)
    for cp in zt:
        cp.start()

    for cp in convs:
        cp.wait_recv()
    for h in range(H):
        cols = slice(h * W, (h + 1) * W)
        acc = convb[my_rows, cols].astype(F32)
        for k in range(1, 8):
            acc = acc + convr[k, :, cols].astype(F32)
        conv_out[pl.ds(h, CL, stride=H), :] = acc

    for cp in zt:
        cp.wait_recv()
    q1, q2 = unpack(add_up(z_t))
    q1 = q1 / n
    q2 = q2 / n
    for h in range(H):
        cols = slice(h * W, (h + 1) * W)
        fgrad[pl.ds(h, CL, stride=H), :] = rstd * (agr[:, cols] - q1 - xh[:, cols] * q2)

    def forward(q, half):
        return remote(gfin.at[half, q], gfin.at[half, q], fw_s.at[q], fw_r.at[q], partner)

    def relay(q, _):
        @pl.when(q != my_q)
        def _():
            remote(gfin.at[core, q], gfin.at[core, q], ag_s.at[0], ag_r.at[q], partner).wait_recv()

        forward(q, core).start()
        return 0

    lax.fori_loop(0, NQ, relay, 0)

    def relayed(q, _):
        forward(q, 1 - core).wait_recv()
        return 0

    lax.fori_loop(0, NQ, relayed, 0)
    for half in range(2):
        for rc in range(6):
            for c in range(4):
                top = (half * 6 + rc) * CH
                kgrad[top:top + CH, c * W:(c + 1) * W] = gfin[half, rc * 4 + c]

    for cp in yst + edges + cots + zst + halos + [swap] + convs + yt + zt:
        cp.wait_send()

    def rs_done(k, _):
        tz, cp = rs_copy(k)

        @pl.when(tz < OWN_Z)
        def _():
            cp.wait_send()

        return 0

    lax.fori_loop(1, 32, rs_done, 0)

    @pl.when(owner)
    def _():
        def given(k, _):
            ag_copy(k).wait_send()
            return 0

        lax.fori_loop(1, 32, given, 0)

    def fw_done(q, _):
        forward(q, core).wait_send()
        return 0

    lax.fori_loop(0, NQ, fw_done, 0)


def per_device(features, gain, bias, kernel, cotangent):
    vmem = pl.BlockSpec(memory_space=pltpu.VMEM)
    dma = pltpu.SemaphoreType.DMA
    conv_out, fgrad, kgrad = pl.pallas_call(
        body,
        out_shape=(
            jax.ShapeDtypeStruct((CL * H, W), F32),
            jax.ShapeDtypeStruct((CL * H, W), F32),
            jax.ShapeDtypeStruct((9 * CL, C), BF16),
        ),
        in_specs=[vmem] * 5,
        out_specs=(vmem,) * 3,
        scratch_shapes=[
            pltpu.VMEM((CL * H, W), F32),
            pltpu.VMEM((CL, S), F32),
            pltpu.VMEM((CL, S), F32),
            pltpu.VMEM((CL, S), F32),
            pltpu.VMEM((9 * CL, S), BF16),
            pltpu.VMEM((C, 9 * CL), BF16),
            pltpu.VMEM((C, S), BF16),
            pltpu.VMEM((C, W), BF16),
            pltpu.VMEM((2 * CL, W), BF16),
            pltpu.VMEM((2, 2 * CL, W), BF16),
            pltpu.VMEM((8, 1, W), F32),
            pltpu.VMEM((8, 1, W), F32),
            pltpu.VMEM((8, 1, W), F32),
            pltpu.VMEM((8, 1, W), F32),
            pltpu.VMEM((C, S), BF16),
            pltpu.VMEM((8, CL, S), BF16),
            pltpu.VMEM((2, NQ, CH, W), F32),
            pltpu.VMEM((NQ, CH, W), BF16),
            pltpu.VMEM((NQ, CH, W), BF16),
            pltpu.VMEM((NQ, CH, W), BF16),
            pltpu.VMEM((32, CH, W), BF16),
            pltpu.VMEM((2, NQ, CH, W), BF16),
            pltpu.VMEM((9 * CL, S), F32),
            pltpu.VMEM((CL, S), F32),
            dma((2,)), dma((2,)),
            dma((8,)), dma((8,)),
            dma((8,)), dma((8,)),
            dma((8,)), dma((8,)),
            dma((8,)), dma((8,)),
            dma((8,)), dma((8,)),
            dma((8,)), dma((8,)),
            dma((8,)), dma((8,)),
            dma((1,)), dma((1,)),
            dma((32,)), dma((32,)),
            dma((32,)), dma((NQ,)),
            dma((NQ,)), dma((NQ,)),
        ],
        compiler_params=pltpu.CompilerParams(
            collective_id=0, has_side_effects=True, vmem_limit_bytes=40 * 1024 * 1024
        ),
        name="strip",
    )(
        features.reshape(CL * H, W),
        gain.reshape(1, CL),
        bias.reshape(1, CL),
        kernel.reshape(9 * CL, C),
        cotangent.reshape(CL * H, W),
    )
    shape = features.shape
    return (
        conv_out.astype(BF16).reshape(shape),
        fgrad.astype(BF16).reshape(shape),
        (kgrad.astype(F32) * (2.0 ** -8)).reshape(kernel.shape),
    )


def solution(mesh):
    in_specs = (
        P("ch", None, None, "lon"),
        P("ch"),
        P("ch"),
        P(None, None, "ch", None),
        P("ch", None, None, "lon"),
    )
    out_specs = (P("ch", None, None, "lon"), P("ch", None, None, "lon"), P(None, None, "ch", None))
    return jax.shard_map(
        per_device, mesh=mesh, in_specs=in_specs, out_specs=out_specs, check_vma=False
    )
```

time: 955 us -> 73.8 us (0.08)
  waiting for transfers between devices: 590 us -> 0 us
  blocking collectives: 290 us -> 0 us
  Pallas kernels: 0 us -> 66.9 us
  matrix products: 29.6 us -> 0 us
  starting transfers between devices: 15.3 us -> 0 us
  between operations: 14 us -> 0.65 us
    psum x1 -> x0, waiting for transfers between devices: 526 us -> none  [per_device(): lax.psum(kern_local, 'lon')]
    psum x2 -> x0, blocking collectives: 290 us -> none  [the longest x1 146 us: per_device(): lax.psum((strip_groups(feature_map, channels_per_group), strip_groups(fea...]
    pallas_call x0 -> x1, Pallas kernels: none -> 66.9 us  [per_device(): pl.pallas_call(body, out_shape=(jax.ShapeDtypeStruct((CL * H, W), F32), j...]
    reduce_scatter x1 -> x0, waiting for transfers between devices: 55.5 us -> none  [per_device(): conv_out = lax.psum_scatter(total, 'ch', scatter_dimension=0, tiled=True)]
    dot_general x27 -> x0, matrix products: 29.6 us -> none  [the longest x9 18.3 us: per_device(): jnp.einsum('co,cfhw->ofhw', sliced[row_off, col_off], patch, preferred_el...]
    ppermute x4 -> x0, starting transfers between devices: 15.2 us -> none  [the longest x2 7.67 us: extended(): lax.ppermute(lax.slice_in_dim(block, 0, width, axis=dim), axis, backward)]
  transfers between devices with their start and end apart: 7 -> 0, of which waited for: 4 -> 0; matrix products, arithmetic and copies ran while one was open for 2% -> 0% of each run, Pallas kernels for 0% -> 0%
where the time goes in v1:
time: 73.8 us; the launch traced here: 73.6 us
  Pallas kernels  66.9 us (91%)
  local copies, waits for them, and re-layouts  4.17 us (6%)
  other arithmetic  1.91 us (3%)
    pallas_call x1, Pallas kernels, per_device(): pl.pallas_call(body, out_shape=(jax.ShapeDtypeStruct((CL * H, W), F32), j...  66.9 us
    unnamed x10, local copies, waits for them, and re-layouts  4.17 us

profile of v1, /device:TPU:1, one launch (start us, length us, event | category | flops | bytes accessed | tf_op | source)
XLA Modules:
  0.0 73.6 jit_solution(15894192539703648485)
XLA Ops:
  0.6 0.0 copy-start
  0.6 1.1 %copy-done = bf16[3,3,64,512]{3,2,1,0:T(8,128)(2,1)S(1)} copy-done((bf16[3,3,64,512]{3,2,1,0:T(8,128)(2,1)S(1)}, bf16[3,3,64,512]{3,2,1,0:T(8,128)(2,1)}, u32[]{:S(2)}) %copy-start) | copy-done | bytes 589848
  1.7 0.0 copy-start.1
  1.7 0.9 %copy-done.1 = bf16[64,1,8,128]{3,2,1,0:T(8,128)(2,1)S(1)} copy-done((bf16[64,1,8,128]{3,2,1,0:T(8,128)(2,1)S(1)}, bf16[64,1,8,128]{3,2,1,0:T(8,128)(2,1)}, u32[]{:S(2)}) %copy-start.1) | copy-done | bytes 131096
  2.6 0.0 copy-start.2
  2.6 0.9 %copy-done.2 = bf16[64,1,8,128]{3,2,1,0:T(8,128)(2,1)S(1)} copy-done((bf16[64,1,8,128]{3,2,1,0:T(8,128)(2,1)S(1)}, bf16[64,1,8,128]{3,2,1,0:T(8,128)(2,1)}, u32[]{:S(2)}) %copy-start.2) | copy-done | bytes 131096
  3.5 0.0 copy-start.3
  3.5 0.7 copy-done.3
  4.2 0.0 copy-start.4
  4.2 0.7 copy-done.4
  4.8 66.9 %strip.1 = (f32[512,128]{1,0:T(8,128)S(1)}, f32[512,128]{1,0:T(8,128)S(1)}, bf16[576,512]{1,0:T(8,128)(2,1)S(1)}) custom-call(bf16[512,128]{1,0:T(8,128)(2,1)S(1)} %bitcast.15, f32[1,64]{1,0:T(1,128)S(1)} %bitcast.17, f32[1,64]{1,0:T(1,128)S(1)} %bitcast.18, bf16[576,512]{1,0:T(8,128)(2,1)S(1)} %bitcast.14, bf16[512,128]{1,0:T(8,128)(2,1)S(1)} %bitcast.16), custom_call_target="tpu_custom_call" | custom-call | tf_op jit(solution)/shard_map/strip/pallas_call | solution.py:398
  71.7 0.7 convert_bitcast_fusion
  72.4 1.2 %convert_multiply_fusion = f32[576,512]{1,0:T(8,128)} fusion(bf16[576,512]{1,0:T(8,128)(2,1)S(1)} %get-tuple-element.8), kind=kLoop, calls=%fused_computation | loop fusion | flops 589824 | bytes 1769472 | tf_op jit(solution)/shard_map/mul | solution.py:460
Async XLA Ops:
  0.6 1.1 %copy-start = (bf16[3,3,64,512]{3,2,1,0:T(8,128)(2,1)S(1)}, bf16[3,3,64,512]{3,2,1,0:T(8,128)(2,1)}, u32[]{:S(2)}) copy-start(bf16[3,3,64,512]{3,2,1,0:T(8,128)(2,1)} %param.8) | copy-start | bytes 1769476
  1.7 0.9 %copy-start.1 = (bf16[64,1,8,128]{3,2,1,0:T(8,128)(2,1)S(1)}, bf16[64,1,8,128]{3,2,1,0:T(8,128)(2,1)}, u32[]{:S(2)}) copy-start(bf16[64,1,8,128]{3,2,1,0:T(8,128)(2,1)} %param.5) | copy-start | bytes 393220
  2.6 0.9 %copy-start.2 = (bf16[64,1,8,128]{3,2,1,0:T(8,128)(2,1)S(1)}, bf16[64,1,8,128]{3,2,1,0:T(8,128)(2,1)}, u32[]{:S(2)}) copy-start(bf16[64,1,8,128]{3,2,1,0:T(8,128)(2,1)} %param.9) | copy-start | bytes 393220
  3.5 0.7 copy-start.3
  4.2 0.7 copy-start.4

commit v2 on v1

v2 whole, which is shorter than its diff:
```python
import functools

import jax
import jax.numpy as jnp
from jax import lax
from jax.experimental import pallas as pl
from jax.experimental.pallas import tpu as pltpu
from jax.sharding import PartitionSpec as P

C = 512
G = 32
CL = 64
H = 8
W = 128
S = H * W
NZ, NY = 8, 4
NQ = 24
CH = 48
FAR = sorted(
    ((dz, dy) for dz in range(NZ) for dy in range(NY) if dz or dy),
    key=lambda o: -(min(o[0], NZ - o[0]) + 2 * min(o[1], NY - o[1])),
)
MESH = pl.DeviceIdType.MESH
F32 = jnp.float32
BF16 = jnp.bfloat16


def body(
    feat_in, gain, bias, w_in, cot_in,
    conv_out, fgrad, kgrad,
    feat, cot, w, in_s, tmp, x2, xh, dact, patch, wt, cotall, halo, edge, edge_in,
    c_st, y_st, z_st, c_t, y_t, z_t,
    convb, convr, convp, convq, g3, gsend, gcore, hb, rsbuf, gfin, zz, agr, conv_f, fg_f,
    edge_s, edge_r, cot_s, cot_r, halo_s, halo_r, st_s, st_r, t_s, t_r,
    conv_s, conv_r, core_s, core_r, rs_s, rs_r, ag_s, ag_r, fw_s, fw_r, kg_s, out_s,
):
    lon = lax.axis_index("lon")
    ch = lax.axis_index("ch")
    z, yc = lon // 8, lon % 8
    yh, core = yc // 2, yc % 2
    x, yl = ch // 2, ch % 2
    n_lon = 64

    def at_lon(d):
        return (lax.rem(lon + d + n_lon, n_lon), ch)

    def at_ch(k):
        return (lon, lax.rem(ch + k, 8))

    def at_x(k):
        return (lon, lax.rem(x + k, 4) * 2 + yl)

    def at_y(k):
        return (z * 8 + lax.rem(yh + k, NY) * 2 + core, ch)

    def at_z(k):
        return (lax.rem(z + k, 8) * 8 + yc, ch)

    partner = (lon + 1 - 2 * core, ch)
    beside = (lon, ch + 1 - 2 * yl)

    def remote(src, dst, ss, rs, dev):
        return pltpu.make_async_remote_copy(
            src_ref=src, dst_ref=dst, send_sem=ss, recv_sem=rs, device_id=dev, device_id_type=MESH
        )

    loads = [
        pltpu.make_async_copy(a, b, in_s.at[i])
        for i, (a, b) in enumerate(((cot_in, cot), (feat_in, feat), (w_in, w)))
    ]
    for cp in loads:
        cp.start()

    barrier = pltpu.get_barrier_semaphore()
    for count, where in ((8, at_ch), (8, at_z), (NY, at_y)):
        for k in range(1, count):
            pl.semaphore_signal(barrier, inc=1, device_id=where(k), device_id_type=MESH)
    for d in (-1, 1):
        pl.semaphore_signal(barrier, inc=1, device_id=at_lon(d), device_id_type=MESH)

    lane = lax.broadcasted_iota(jnp.int32, (CL, W), 1)
    group = lax.broadcasted_iota(jnp.int32, (CL, W), 0) // 16

    my_rows = pl.ds(pl.multiple_of(ch * CL, CL), CL)

    loads[0].wait()
    tmp[...] = cot[...].astype(F32)
    e = jnp.zeros((CL, W), F32)
    for h in range(H):
        row = tmp[pl.ds(h, CL, stride=H), :]
        cotall[my_rows, h * W:(h + 1) * W] = row.astype(BF16)
        e = jnp.where(lane == h, row[:, W - 1:W], e)
        e = jnp.where(lane == H + h, row[:, 0:1], e)
    edge[0:CL, :] = e.astype(BF16)
    loads[1].wait()
    tmp[...] = feat[...].astype(F32)
    e = jnp.zeros((CL, W), F32)
    total = jnp.zeros((CL, W), F32)
    total2 = jnp.zeros((CL, W), F32)
    for h in range(H):
        row = tmp[pl.ds(h, CL, stride=H), :]
        x2[:, h * W:(h + 1) * W] = row
        total += row
        total2 += row * row
        e = jnp.where(lane == h, row[:, W - 1:W], e)
        e = jnp.where(lane == H + h, row[:, 0:1], e)
    edge[CL:2 * CL, :] = e.astype(BF16)

    def pack(a, b):
        a = jnp.sum(a, axis=1, keepdims=True)
        b = jnp.sum(b, axis=1, keepdims=True)
        both = jnp.where(lane == group, a, 0.0) + jnp.where(lane == group + 4, b, 0.0)
        return jnp.sum(both, axis=0, keepdims=True)

    def unpack(vec):
        full = jnp.broadcast_to(vec, (CL, W))
        a = jnp.sum(jnp.where(lane == group, full, 0.0), axis=1, keepdims=True)
        b = jnp.sum(jnp.where(lane == group + 4, full, 0.0), axis=1, keepdims=True)
        return a, b

    def column(ref):
        r = lax.broadcasted_iota(jnp.int32, (CL, CL), 0)
        c = lax.broadcasted_iota(jnp.int32, (CL, CL), 1)
        return jnp.sum(jnp.where(r == c, jnp.broadcast_to(ref[...], (CL, CL)), 0.0), axis=1, keepdims=True)

    def rounds(bufs, ss, rs):
        def sends(buf, count, base, where):
            return [
                remote(buf.at[0], buf.at[k], ss.at[base + k], rs.at[base + k], where(k))
                for k in range(1, count)
            ]

        return (
            sends(bufs[0], 2, 0, lambda k: partner),
            sends(bufs[1], NY, 2, at_y),
            sends(bufs[2], NZ, 6, at_z),
        )

    def start(copies):
        for cp in copies:
            cp.start()

    def arrive(copies):
        for cp in copies:
            cp.wait_recv()

    def add_up(buf):
        acc = buf[0]
        for k in range(1, buf.shape[0]):
            acc = acc + buf[k]
        return acc

    c_st[0] = pack(total, total2)
    pl.semaphore_wait(barrier, 19)

    st = rounds((c_st, y_st, z_st), st_s, st_r)
    start(st[0])
    edges = [
        remote(edge, edge_in.at[0], edge_s.at[0], edge_r.at[0], at_lon(1)),
        remote(edge, edge_in.at[1], edge_s.at[1], edge_r.at[1], at_lon(-1)),
    ]
    start(edges)
    its_rows = pl.ds(pl.multiple_of((ch + 1 - 2 * yl) * CL, CL), CL)
    cot_pair = [remote(cotall.at[my_rows], cotall.at[my_rows], cot_s.at[0], cot_r.at[0], beside)]
    cot_mine = [
        remote(cotall.at[my_rows], cotall.at[my_rows], cot_s.at[k], cot_r.at[k], at_x(k))
        for k in (1, 3, 2)
    ]
    cot_its = [
        remote(cotall.at[its_rows], cotall.at[its_rows], cot_s.at[3 + k], cot_r.at[3 + k], at_x(k))
        for k in (1, 3, 2)
    ]
    start(cot_pair + cot_mine)
    arrive(st[0])
    y_st[0] = add_up(c_st)
    start(st[1])

    loads[2].wait()
    for i in range(4):
        wt[:, i * 128:(i + 1) * 128] = w[i * 128:(i + 1) * 128, :].astype(F32).T.astype(BF16)
    wt[:, 512:576] = w[512:576, :].astype(F32).T.astype(BF16)

    arrive(cot_pair)
    start(cot_its)
    arrive(st[1])
    z_st[0] = add_up(y_st)
    start(st[2])

    arrive(edges)
    lane2 = lax.broadcasted_iota(jnp.int32, (2 * CL, W), 1)
    rim = jnp.where(lane2 < H, edge_in[0].astype(F32), edge_in[1].astype(F32))
    halo[my_rows, :] = rim[0:CL].astype(BF16)
    halos = [
        remote(halo.at[my_rows], halo.at[my_rows], halo_s.at[k], halo_r.at[k], at_ch(k))
        for k in range(1, 8)
    ]
    start(halos)

    gain_c = column(gain)
    bias_c = column(bias)
    n = float(16 * H * W * n_lon)
    zero = jnp.zeros((192, W), BF16)
    patch[0:192, 0:W] = zero
    patch[384:576, S - W:S] = zero

    arrive(st[2])
    m1, m2 = unpack(add_up(z_st))
    mean = m1 / n
    var = m2 / n - mean * mean
    rstd = 1.0 / jnp.sqrt(var + 1e-06)

    rim_pre = (rim[CL:2 * CL] - mean) * rstd * gain_c + bias_c
    rim_act = rim_pre * jax.nn.sigmoid(rim_pre)
    for h in range(H):
        cols = slice(h * W, (h + 1) * W)
        norm = (x2[:, cols] - mean) * rstd
        pre = norm * gain_c + bias_c
        sig = jax.nn.sigmoid(pre)
        xh[:, cols] = norm
        dact[:, cols] = sig * (1.0 + pre * (1.0 - sig)) * gain_c
        act = pre * sig
        left = jnp.where(lane == 0, rim_act[:, h:h + 1], pltpu.roll(act, 1, 1))
        right = jnp.where(lane == W - 1, rim_act[:, H + h:H + h + 1], pltpu.roll(act, W - 1, 1))
        for s, v in enumerate((left, act, right)):
            v = v.astype(BF16)
            for r in range(3):
                to = h + 1 - r
                if 0 <= to < H:
                    patch[r * 192 + s * CL:r * 192 + (s + 1) * CL, to * W:(to + 1) * W] = v

    my_j = lax.rem(yh - z + 8, 4)
    my_q = my_j * NZ + z
    owner = my_j < 3

    def to(offset):
        tz, ty = lax.rem(z + offset[0], NZ), lax.rem(yh + offset[1], NY)
        j = lax.rem(ty - tz + 8, 4)
        return j < 3, lax.min(j, 2) * NZ + tz, (tz * 8 + ty * 2 + core, ch)

    def swap(i):
        return remote(gsend.at[i], gcore.at[i], core_s.at[i], core_r.at[i], partner)

    def rs_copy(i):
        takes, q, dev = to(FAR[i])
        return takes, q, remote(hb.at[q], rsbuf.at[i], rs_s.at[i], rs_r.at[i], dev)

    def send_sums(i):
        lc = lax.rem(x + (0, 1, 3, 2)[i], 4)
        swap(i).wait_recv()
        for rc in range(6):
            hb[lc * 6 + rc] = (g3[core, i, rc] + gcore[i, rc].astype(F32)).astype(BF16)
        for k in range(31):
            takes, q, cp = rs_copy(k)

            @pl.when(takes & (q >= lc * 6) & (q < lc * 6 + 6))
            def _(cp=cp):
                cp.start()

    for i in range(4):
        d = (0, 1, 3, 2)[i]
        if d:
            remote(cotall.at[my_rows], cotall.at[my_rows], cot_s.at[0], cot_r.at[4 - d], beside).wait_recv()
            remote(cotall.at[my_rows], cotall.at[my_rows], cot_s.at[0], cot_r.at[7 - d], beside).wait_recv()
        rows = pl.ds(pl.multiple_of(lax.rem(x + d, 4) * W, W), W)
        part = lax.dot_general(
            patch[...], cotall[rows, :], (((1,), (1,)), ((), ())), preferred_element_type=F32
        )
        for rc in range(12):
            g3[rc // 6, i, rc % 6] = part[rc * CH:(rc + 1) * CH]
        gsend[i] = g3[1 - core, i].astype(BF16)
        swap(i).start()
        if i:
            send_sums(i - 1)
    send_sums(3)

    def conv_step(i, _):
        cols = pl.ds(pl.multiple_of(i * 256, 256), 256)
        convb[:, cols] = jnp.dot(wt[...], patch[:, cols], preferred_element_type=F32).astype(BF16)
        return 0

    lax.fori_loop(0, 4, conv_step, 0)

    def pair_rows(k):
        return pl.ds(pl.multiple_of(lax.rem(x + k, 4) * W, W), W)

    convs = [
        remote(convb.at[pair_rows(k)], convr.at[k - 1], conv_s.at[k], conv_r.at[k], at_x(k))
        for k in (2, 1, 3)
    ]
    start(convs)

    arrive(halos)

    def z_step(i, _):
        cols = pl.ds(pl.multiple_of(i * 256, 256), 256)
        zz[:, cols] = jnp.dot(w[...], cotall[:, cols], preferred_element_type=F32)
        return 0

    lax.fori_loop(0, 4, z_step, 0)
    zh = jnp.dot(w[...], halo[...], preferred_element_type=F32)

    def zrows(r, s):
        return slice(r * 192 + s * CL, r * 192 + (s + 1) * CL)

    def rim_sum(s):
        up = jnp.where((lane % H) < H - 1, pltpu.roll(zh[zrows(0, s)], W - 1, 1), 0.0)
        down = jnp.where((lane % H) > 0, pltpu.roll(zh[zrows(2, s)], 1, 1), 0.0)
        return up + zh[zrows(1, s)] + down

    rim0, rim2 = rim_sum(0), rim_sum(2)
    t1 = jnp.zeros((CL, W), F32)
    t2 = jnp.zeros((CL, W), F32)
    for h in range(H):
        u = []
        for s in range(3):
            acc = zz[zrows(1, s), h * W:(h + 1) * W]
            if h + 1 < H:
                acc = acc + zz[zrows(0, s), (h + 1) * W:(h + 2) * W]
            if h >= 1:
                acc = acc + zz[zrows(2, s), (h - 1) * W:h * W]
            u.append(acc)
        agrad = u[1]
        agrad = agrad + jnp.where(lane == W - 1, rim0[:, H + h:H + h + 1], pltpu.roll(u[0], W - 1, 1))
        agrad = agrad + jnp.where(lane == 0, rim2[:, h:h + 1], pltpu.roll(u[2], 1, 1))
        cols = slice(h * W, (h + 1) * W)
        ng = agrad * dact[:, cols]
        agr[:, cols] = ng
        t1 += ng
        t2 += ng * xh[:, cols]
    c_t[0] = pack(t1, t2)
    tt = rounds((c_t, y_t, z_t), t_s, t_r)
    start(tt[0])
    arrive(tt[0])
    y_t[0] = add_up(c_t)
    start(tt[1])

    def ag_copy(k):
        q = lax.min(my_j, 2) * NZ + z
        return remote(gfin.at[core, q], gfin.at[core, q], ag_s.at[k], ag_r.at[q], to(FAR[k])[2])

    @pl.when(owner)
    def _():
        acc = hb[my_q].astype(F32)
        for k in reversed(range(31)):
            rs_copy(k)[2].wait_recv()
            acc = acc + rsbuf[k].astype(F32)
        gfin[core, my_q] = acc.astype(BF16)
        for k in range(31):
            ag_copy(k).start()

    arrive(tt[1])
    z_t[0] = add_up(y_t)
    start(tt[2])

    arrive(convs)
    for half in range(2):
        for h in range(H):
            cols = slice(h * W, (h + 1) * W)
            top = pl.ds(pl.multiple_of(x * W + half * CL, CL), CL)
            acc = convb[top, cols].astype(F32)
            for k in range(3):
                acc = acc + convr[k, half * CL:(half + 1) * CL, cols].astype(F32)
            convp[half, :, cols] = acc.astype(BF16)
    conv_pair = remote(convp.at[1 - yl], convq, conv_s.at[0], conv_r.at[0], beside)
    conv_pair.start()

    arrive(tt[2])
    q1, q2 = unpack(add_up(z_t))
    q1 = q1 / n
    q2 = q2 / n
    for h in range(H):
        cols = slice(h * W, (h + 1) * W)
        fg_f[pl.ds(h, CL, stride=H), :] = rstd * (agr[:, cols] - q1 - xh[:, cols] * q2)

    outs = [
        pltpu.make_async_copy(fg_f, fgrad, out_s.at[0]),
        pltpu.make_async_copy(conv_f, conv_out, out_s.at[1]),
    ]
    outs[0].start()

    arrive([conv_pair])
    for h in range(H):
        cols = slice(h * W, (h + 1) * W)
        conv_f[pl.ds(h, CL, stride=H), :] = convp[yl, :, cols].astype(F32) + convq[:, cols].astype(F32)
    outs[1].start()

    def forward(q, half):
        return remote(gfin.at[half, q], gfin.at[half, q], fw_s.at[q], fw_r.at[q], partner)

    def store(q, half):
        rows = pl.ds(pl.multiple_of((half * 6 + lax.rem(q, 6)) * CH, CH), CH)
        cols = pl.ds(pl.multiple_of(q // 6 * W, W), W)
        return pltpu.make_async_copy(gfin.at[half, q], kgrad.at[rows, cols], kg_s.at[half, q])

    def turn(i):
        return lax.rem(i + x * 6, NQ)

    def relay(i, _):
        q = turn(i)

        @pl.when(q != my_q)
        def _():
            remote(gfin.at[core, q], gfin.at[core, q], ag_s.at[0], ag_r.at[q], partner).wait_recv()

        forward(q, core).start()
        store(q, core).start()
        return 0

    lax.fori_loop(0, NQ, relay, 0)

    def relayed(i, _):
        q = turn(i)
        forward(q, 1 - core).wait_recv()
        store(q, 1 - core).start()
        return 0

    lax.fori_loop(0, NQ, relayed, 0)

    for cp in edges + cot_pair + cot_mine + cot_its + halos + convs + [conv_pair]:
        cp.wait_send()
    for part in st + tt:
        for cp in part:
            cp.wait_send()
    for i in range(4):
        swap(i).wait_send()
    for k in range(31):
        takes, _, cp = rs_copy(k)

        @pl.when(takes)
        def _(cp=cp):
            cp.wait_send()

    @pl.when(owner)
    def _():
        for k in range(31):
            ag_copy(k).wait_send()

    for cp in outs:
        cp.wait()

    def done(q, _):
        forward(q, core).wait_send()
        store(q, core).wait()
        store(q, 1 - core).wait()
        return 0

    lax.fori_loop(0, NQ, done, 0)


def per_device(features, gain, bias, kernel, cotangent):
    vmem = pl.BlockSpec(memory_space=pltpu.VMEM)
    hbm = pl.BlockSpec(memory_space=pltpu.HBM)
    dma = pltpu.SemaphoreType.DMA
    conv_out, fgrad, kgrad = pl.pallas_call(
        body,
        out_shape=(
            jax.ShapeDtypeStruct((CL * H, W), F32),
            jax.ShapeDtypeStruct((CL * H, W), F32),
            jax.ShapeDtypeStruct((9 * CL, C), BF16),
        ),
        in_specs=[hbm, vmem, vmem, hbm, hbm],
        out_specs=(hbm,) * 3,
        scratch_shapes=[
            pltpu.VMEM((CL * H, W), BF16),
            pltpu.VMEM((CL * H, W), BF16),
            pltpu.VMEM((9 * CL, C), BF16),
            dma((3,)),
            pltpu.VMEM((CL * H, W), F32),
            pltpu.VMEM((CL, S), F32),
            pltpu.VMEM((CL, S), F32),
            pltpu.VMEM((CL, S), F32),
            pltpu.VMEM((9 * CL, S), BF16),
            pltpu.VMEM((C, 9 * CL), BF16),
            pltpu.VMEM((C, S), BF16),
            pltpu.VMEM((C, W), BF16),
            pltpu.VMEM((2 * CL, W), BF16),
            pltpu.VMEM((2, 2 * CL, W), BF16),
            pltpu.VMEM((2, 1, W), F32),
            pltpu.VMEM((NY, 1, W), F32),
            pltpu.VMEM((NZ, 1, W), F32),
            pltpu.VMEM((2, 1, W), F32),
            pltpu.VMEM((NY, 1, W), F32),
            pltpu.VMEM((NZ, 1, W), F32),
            pltpu.VMEM((C, S), BF16),
            pltpu.VMEM((3, 2 * CL, S), BF16),
            pltpu.VMEM((2, CL, S), BF16),
            pltpu.VMEM((CL, S), BF16),
            pltpu.VMEM((2, 4, 6, CH, W), F32),
            pltpu.VMEM((4, 6, CH, W), BF16),
            pltpu.VMEM((4, 6, CH, W), BF16),
            pltpu.VMEM((NQ, CH, W), BF16),
            pltpu.VMEM((31, CH, W), BF16),
            pltpu.VMEM((2, NQ, CH, W), BF16),
            pltpu.VMEM((9 * CL, S), F32),
            pltpu.VMEM((CL, S), F32),
            pltpu.VMEM((CL * H, W), F32),
            pltpu.VMEM((CL * H, W), F32),
            dma((2,)), dma((2,)),
            dma((7,)), dma((7,)),
            dma((8,)), dma((8,)),
            dma((14,)), dma((14,)),
            dma((14,)), dma((14,)),
            dma((4,)), dma((4,)),
            dma((4,)), dma((4,)),
            dma((31,)), dma((31,)),
            dma((31,)), dma((NQ,)),
            dma((NQ,)), dma((NQ,)),
            dma((2, NQ)),
            dma((2,)),
        ],
        compiler_params=pltpu.CompilerParams(
            collective_id=0, has_side_effects=True, vmem_limit_bytes=62 * 1024 * 1024
        ),
        name="strip",
    )(
        features.reshape(CL * H, W),
        gain.reshape(1, CL),
        bias.reshape(1, CL),
        kernel.reshape(9 * CL, C),
        cotangent.reshape(CL * H, W),
    )
    shape = features.shape
    return (
        conv_out.astype(BF16).reshape(shape),
        fgrad.astype(BF16).reshape(shape),
        (kgrad.astype(F32) * (2.0 ** -8)).reshape(kernel.shape),
    )


def solution(mesh):
    in_specs = (
        P("ch", None, None, "lon"),
        P("ch"),
        P("ch"),
        P(None, None, "ch", None),
        P("ch", None, None, "lon"),
    )
    out_specs = (P("ch", None, None, "lon"), P("ch", None, None, "lon"), P(None, None, "ch", None))
    return jax.shard_map(
        per_device, mesh=mesh, in_specs=in_specs, out_specs=out_specs, check_vma=False
    )
```

time: 73.8 us -> 61.7 us (0.84)
  Pallas kernels: 66.9 us -> 57.9 us
  local copies, waits for them, and re-layouts: 4.17 us -> 0.01 us
  other arithmetic: 1.91 us -> 3 us
    pallas_call x1, Pallas kernels: 66.9 us -> 57.9 us  [per_device(): pl.pallas_call(body, out_shape=(jax.ShapeDtypeStruct((CL * H, W), F32), j...]
    unnamed x10 -> x2, local copies, waits for them, and re-layouts: 4.17 us -> 0.01 us
    unnamed x1, other arithmetic: 0.73 us -> 1.82 us
where the time goes in v2:
time: 61.7 us; the launch traced here: 61.5 us
  Pallas kernels  57.9 us (94%)
  other arithmetic  3 us (5%)
  between operations  0.65 us (1%)
    pallas_call x1, Pallas kernels, per_device(): pl.pallas_call(body, out_shape=(jax.ShapeDtypeStruct((CL * H, W), F32), j...  57.9 us
    unnamed x1, other arithmetic  1.82 us

profile of v2, /device:TPU:1, one launch (start us, length us, event | category | flops | bytes accessed | tf_op | source)
XLA Modules:
  0.0 61.5 jit_solution(16477252330046357082)
XLA Ops:
  0.6 57.9 %strip.1 = (f32[512,128]{1,0:T(8,128)}, f32[512,128]{1,0:T(8,128)}, bf16[576,512]{1,0:T(8,128)(2,1)}) custom-call(bf16[512,128]{1,0:T(8,128)(2,1)} %bitcast.16, f32[1,64]{1,0:T(1,128)} %bitcast.18, f32[1,64]{1,0:T(1,128)} %bitcast.19, bf16[576,512]{1,0:T(8,128)(2,1)} %bitcast.15, bf16[512,128]{1,0:T(8,128)(2,1)} %bitcast.17), custom_call_target="tpu_custom_call" | custom-call | tf_op jit(solution)/shard_map/strip/pallas_call | solution.py:454
  58.5 0.0 copy-start
  58.5 1.8 %convert_bitcast_fusion = (bf16[64,1,8,128]{3,2,1,0:T(8,128)(2,1)}, bf16[64,1,8,128]{3,2,1,0:T(8,128)(2,1)}) fusion(f32[512,128]{1,0:T(8,128)} %get-tuple-element.7, f32[512,128]{1,0:T(8,128)} %get-tuple-element.6), kind=kLoop, calls=%fused_computation.1 | loop fusion | flops 131072 | bytes 786432
  60.4 0.0 copy-done
  60.4 1.2 %convert_multiply_fusion = f32[576,512]{1,0:T(8,128)} fusion(bf16[576,512]{1,0:T(8,128)(2,1)S(1)} %copy-done), kind=kLoop, calls=%fused_computation | loop fusion | flops 589824 | bytes 1769472 | tf_op jit(solution)/shard_map/mul | solution.py:526
Async XLA Ops:
  58.5 1.8 %copy-start = (bf16[576,512]{1,0:T(8,128)(2,1)S(1)}, bf16[576,512]{1,0:T(8,128)(2,1)}, u32[]{:S(2)}) copy-start(bf16[576,512]{1,0:T(8,128)(2,1)} %get-tuple-element.8) | copy-start | bytes 1769476

commit v3 on v2

--- a/solution.py
+++ b/solution.py
@@ -16,9 +16,9 @@
 NZ, NY = 8, 4
 NQ = 24
 CH = 48
-FAR = sorted(
+NEAR = sorted(
     ((dz, dy) for dz in range(NZ) for dy in range(NY) if dz or dy),
-    key=lambda o: -(min(o[0], NZ - o[0]) + 2 * min(o[1], NY - o[1])),
+    key=lambda o: min(o[0], NZ - o[0]) + 2 * min(o[1], NY - o[1]),
 )
 MESH = pl.DeviceIdType.MESH
 F32 = jnp.float32
@@ -30,7 +30,7 @@
     conv_out, fgrad, kgrad,
     feat, cot, w, in_s, tmp, x2, xh, dact, patch, wt, cotall, halo, edge, edge_in,
     c_st, y_st, z_st, c_t, y_t, z_t,
-    convb, convr, convp, convq, g3, gsend, gcore, hb, rsbuf, gfin, zz, agr, conv_f, fg_f,
+    convb, convr, convp, convq, convown, g3, gsend, gcore, hb, rsbuf, gfin, zz, agr, conv_f, fg_f,
     edge_s, edge_r, cot_s, cot_r, halo_s, halo_r, st_s, st_r, t_s, t_r,
     conv_s, conv_r, core_s, core_r, rs_s, rs_r, ag_s, ag_r, fw_s, fw_r, kg_s, out_s,
 ):
@@ -66,7 +66,7 @@
 
     loads = [
         pltpu.make_async_copy(a, b, in_s.at[i])
-        for i, (a, b) in enumerate(((cot_in, cot), (feat_in, feat), (w_in, w)))
+        for i, (a, b) in enumerate(((feat_in, feat), (cot_in, cot), (w_in, w)))
     ]
     for cp in loads:
         cp.start()
@@ -84,17 +84,7 @@
     my_rows = pl.ds(pl.multiple_of(ch * CL, CL), CL)
 
     loads[0].wait()
-    tmp[...] = cot[...].astype(F32)
-    e = jnp.zeros((CL, W), F32)
-    for h in range(H):
-        row = tmp[pl.ds(h, CL, stride=H), :]
-        cotall[my_rows, h * W:(h + 1) * W] = row.astype(BF16)
-        e = jnp.where(lane == h, row[:, W - 1:W], e)
-        e = jnp.where(lane == H + h, row[:, 0:1], e)
-    edge[0:CL, :] = e.astype(BF16)
-    loads[1].wait()
     tmp[...] = feat[...].astype(F32)
-    e = jnp.zeros((CL, W), F32)
     total = jnp.zeros((CL, W), F32)
     total2 = jnp.zeros((CL, W), F32)
     for h in range(H):
@@ -102,9 +92,6 @@
         x2[:, h * W:(h + 1) * W] = row
         total += row
         total2 += row * row
-        e = jnp.where(lane == h, row[:, W - 1:W], e)
-        e = jnp.where(lane == H + h, row[:, 0:1], e)
-    edge[CL:2 * CL, :] = e.astype(BF16)
 
     def pack(a, b):
         a = jnp.sum(a, axis=1, keepdims=True)
@@ -131,9 +118,9 @@
             ]
 
         return (
-            sends(bufs[0], 2, 0, lambda k: partner),
-            sends(bufs[1], NY, 2, at_y),
-            sends(bufs[2], NZ, 6, at_z),
+            sends(bufs[0], NZ, 0, at_z),
+            sends(bufs[1], 2, 8, lambda k: partner),
+            sends(bufs[2], NY, 10, at_y),
         )
 
     def start(copies):
@@ -150,31 +137,44 @@
             acc = acc + buf[k]
         return acc
 
-    c_st[0] = pack(total, total2)
+    z_st[0] = pack(total, total2)
+    loads[1].wait()
+    tmp[...] = cot[...].astype(F32)
+    for h in range(H):
+        cotall[my_rows, h * W:(h + 1) * W] = tmp[pl.ds(h, CL, stride=H), :].astype(BF16)
     pl.semaphore_wait(barrier, 19)
 
-    st = rounds((c_st, y_st, z_st), st_s, st_r)
+    st = rounds((z_st, c_st, y_st), st_s, st_r)
     start(st[0])
-    edges = [
-        remote(edge, edge_in.at[0], edge_s.at[0], edge_r.at[0], at_lon(1)),
-        remote(edge, edge_in.at[1], edge_s.at[1], edge_r.at[1], at_lon(-1)),
-    ]
-    start(edges)
     its_rows = pl.ds(pl.multiple_of((ch + 1 - 2 * yl) * CL, CL), CL)
     cot_pair = [remote(cotall.at[my_rows], cotall.at[my_rows], cot_s.at[0], cot_r.at[0], beside)]
     cot_mine = [
         remote(cotall.at[my_rows], cotall.at[my_rows], cot_s.at[k], cot_r.at[k], at_x(k))
-        for k in (1, 3, 2)
+        for k in (2, 1, 3)
     ]
     cot_its = [
         remote(cotall.at[its_rows], cotall.at[its_rows], cot_s.at[3 + k], cot_r.at[3 + k], at_x(k))
-        for k in (1, 3, 2)
-    ]
+        for k in (1, 3)
+    ]
+    two_rows = pl.ds(pl.multiple_of((lax.rem(x + 2, 4) * 2 + yl) * CL, CL), CL)
+    cot_two = [remote(cotall.at[two_rows], cotall.at[two_rows], cot_s.at[5], cot_r.at[5], beside)]
     start(cot_pair + cot_mine)
-    arrive(st[0])
-    y_st[0] = add_up(c_st)
-    start(st[1])
-
+
+    for part, src in ((0, None), (1, x2)):
+        e = jnp.zeros((CL, W), F32)
+        for h in range(H):
+            if src is None:
+                row = cotall[my_rows, h * W:(h + 1) * W].astype(F32)
+            else:
+                row = src[:, h * W:(h + 1) * W]
+            e = jnp.where(lane == h, row[:, W - 1:W], e)
+            e = jnp.where(lane == H + h, row[:, 0:1], e)
+        edge[part * CL:(part + 1) * CL, :] = e.astype(BF16)
+    edges = [
+        remote(edge, edge_in.at[0], edge_s.at[0], edge_r.at[0], at_lon(1)),
+        remote(edge, edge_in.at[1], edge_s.at[1], edge_r.at[1], at_lon(-1)),
+    ]
+    start(edges)
     loads[2].wait()
     for i in range(4):
         wt[:, i * 128:(i + 1) * 128] = w[i * 128:(i + 1) * 128, :].astype(F32).T.astype(BF16)
@@ -182,9 +182,14 @@
 
     arrive(cot_pair)
     start(cot_its)
+    arrive(st[0])
+    c_st[0] = add_up(z_st)
+    start(st[1])
     arrive(st[1])
-    z_st[0] = add_up(y_st)
+    y_st[0] = add_up(c_st)
     start(st[2])
+    arrive(cot_mine[:1])
+    start(cot_two)
 
     arrive(edges)
     lane2 = lax.broadcasted_iota(jnp.int32, (2 * CL, W), 1)
@@ -204,7 +209,7 @@
     patch[384:576, S - W:S] = zero
 
     arrive(st[2])
-    m1, m2 = unpack(add_up(z_st))
+    m1, m2 = unpack(add_up(y_st))
     mean = m1 / n
     var = m2 / n - mean * mean
     rstd = 1.0 / jnp.sqrt(var + 1e-06)
@@ -232,34 +237,34 @@
     my_q = my_j * NZ + z
     owner = my_j < 3
 
-    def to(offset):
-        tz, ty = lax.rem(z + offset[0], NZ), lax.rem(yh + offset[1], NY)
-        j = lax.rem(ty - tz + 8, 4)
-        return j < 3, lax.min(j, 2) * NZ + tz, (tz * 8 + ty * 2 + core, ch)
+    def to(tz, ty):
+        return (tz * 8 + ty * 2 + core, ch)
 
     def swap(i):
         return remote(gsend.at[i], gcore.at[i], core_s.at[i], core_r.at[i], partner)
-
-    def rs_copy(i):
-        takes, q, dev = to(FAR[i])
-        return takes, q, remote(hb.at[q], rsbuf.at[i], rs_s.at[i], rs_r.at[i], dev)
 
     def send_sums(i):
         lc = lax.rem(x + (0, 1, 3, 2)[i], 4)
         swap(i).wait_recv()
         for rc in range(6):
             hb[lc * 6 + rc] = (g3[core, i, rc] + gcore[i, rc].astype(F32)).astype(BF16)
-        for k in range(31):
-            takes, q, cp = rs_copy(k)
-
-            @pl.when(takes & (q >= lc * 6) & (q < lc * 6 + 6))
-            def _(cp=cp):
-                cp.start()
+        for rc in range(6):
+            q = lc * 6 + rc
+            tz = lax.rem(q, NZ)
+            ty = lax.rem(q // NZ + tz, NY)
+            slot = lax.rem(tz - z + NZ, NZ) * NY + lax.rem(ty - yh + NY, NY)
+
+            @pl.when(q != my_q)
+            def _(q=q, tz=tz, ty=ty, slot=slot):
+                remote(hb.at[q], rsbuf.at[slot], rs_s.at[0], rs_r.at[slot], to(tz, ty)).start()
 
     for i in range(4):
         d = (0, 1, 3, 2)[i]
         if d:
-            remote(cotall.at[my_rows], cotall.at[my_rows], cot_s.at[0], cot_r.at[4 - d], beside).wait_recv()
+            if d != 2:
+                remote(
+                    cotall.at[my_rows], cotall.at[my_rows], cot_s.at[0], cot_r.at[4 - d], beside
+                ).wait_recv()
             remote(cotall.at[my_rows], cotall.at[my_rows], cot_s.at[0], cot_r.at[7 - d], beside).wait_recv()
         rows = pl.ds(pl.multiple_of(lax.rem(x + d, 4) * W, W), W)
         part = lax.dot_general(
@@ -275,10 +280,14 @@
 
     def conv_step(i, _):
         cols = pl.ds(pl.multiple_of(i * 256, 256), 256)
-        convb[:, cols] = jnp.dot(wt[...], patch[:, cols], preferred_element_type=F32).astype(BF16)
+        part = jnp.dot(wt[...], patch[:, cols], preferred_element_type=F32)
+        zz[0:C, cols] = part
+        convb[:, cols] = part.astype(BF16)
         return 0
 
     lax.fori_loop(0, 4, conv_step, 0)
+    for half in range(2):
+        convown[half] = zz[pl.ds(pl.multiple_of(x * W + half * CL, CL), CL), :]
 
     def pair_rows(k):
         return pl.ds(pl.multiple_of(lax.rem(x + k, 4) * W, W), W)
@@ -327,45 +336,50 @@
         agr[:, cols] = ng
         t1 += ng
         t2 += ng * xh[:, cols]
-    c_t[0] = pack(t1, t2)
-    tt = rounds((c_t, y_t, z_t), t_s, t_r)
+    z_t[0] = pack(t1, t2)
+    tt = rounds((z_t, c_t, y_t), t_s, t_r)
     start(tt[0])
-    arrive(tt[0])
-    y_t[0] = add_up(c_t)
-    start(tt[1])
-
-    def ag_copy(k):
+
+    def ag_copy(dz, dy):
         q = lax.min(my_j, 2) * NZ + z
-        return remote(gfin.at[core, q], gfin.at[core, q], ag_s.at[k], ag_r.at[q], to(FAR[k])[2])
+        dev = to(lax.rem(z + dz, NZ), lax.rem(yh + dy, NY))
+        return remote(gfin.at[core, q], gfin.at[core, q], ag_s.at[0], ag_r.at[q], dev)
 
     @pl.when(owner)
     def _():
         acc = hb[my_q].astype(F32)
-        for k in reversed(range(31)):
-            rs_copy(k)[2].wait_recv()
-            acc = acc + rsbuf[k].astype(F32)
+        for dz, dy in NEAR:
+            slot = dz * NY + dy
+            remote(hb.at[0], rsbuf.at[slot], rs_s.at[0], rs_r.at[slot], partner).wait_recv()
+            acc = acc + rsbuf[slot].astype(F32)
         gfin[core, my_q] = acc.astype(BF16)
-        for k in range(31):
-            ag_copy(k).start()
-
+        for dz, dy in reversed(NEAR):
+            ag_copy(dz, dy).start()
+
+    arrive(tt[0])
+    c_t[0] = add_up(z_t)
+    start(tt[1])
     arrive(tt[1])
-    z_t[0] = add_up(y_t)
+    y_t[0] = add_up(c_t)
     start(tt[2])
 
     arrive(convs)
-    for half in range(2):
-        for h in range(H):
-            cols = slice(h * W, (h + 1) * W)
-            top = pl.ds(pl.multiple_of(x * W + half * CL, CL), CL)
-            acc = convb[top, cols].astype(F32)
-            for k in range(3):
-                acc = acc + convr[k, half * CL:(half + 1) * CL, cols].astype(F32)
-            convp[half, :, cols] = acc.astype(BF16)
-    conv_pair = remote(convp.at[1 - yl], convq, conv_s.at[0], conv_r.at[0], beside)
+
+    def pair_sum(half, h):
+        cols = slice(h * W, (h + 1) * W)
+        acc = convown[half, :, cols]
+        for k in range(3):
+            rows = pl.ds(pl.multiple_of(half * CL, CL), CL)
+            acc = acc + convr[k, rows, cols].astype(F32)
+        return acc
+
+    for h in range(H):
+        convp[:, h * W:(h + 1) * W] = pair_sum(1 - yl, h).astype(BF16)
+    conv_pair = remote(convp, convq, conv_s.at[0], conv_r.at[0], beside)
     conv_pair.start()
 
     arrive(tt[2])
-    q1, q2 = unpack(add_up(z_t))
+    q1, q2 = unpack(add_up(y_t))
     q1 = q1 / n
     q2 = q2 / n
     for h in range(H):
@@ -381,70 +395,62 @@
     arrive([conv_pair])
     for h in range(H):
         cols = slice(h * W, (h + 1) * W)
-        conv_f[pl.ds(h, CL, stride=H), :] = convp[yl, :, cols].astype(F32) + convq[:, cols].astype(F32)
+        conv_f[pl.ds(h, CL, stride=H), :] = pair_sum(yl, h) + convq[:, cols].astype(F32)
     outs[1].start()
 
-    def forward(q, half):
-        return remote(gfin.at[half, q], gfin.at[half, q], fw_s.at[q], fw_r.at[q], partner)
-
-    def store(q, half):
-        rows = pl.ds(pl.multiple_of((half * 6 + lax.rem(q, 6)) * CH, CH), CH)
-        cols = pl.ds(pl.multiple_of(q // 6 * W, W), W)
-        return pltpu.make_async_copy(gfin.at[half, q], kgrad.at[rows, cols], kg_s.at[half, q])
-
-    def turn(i):
-        return lax.rem(i + x * 6, NQ)
-
-    def relay(i, _):
-        q = turn(i)
-
-        @pl.when(q != my_q)
-        def _():
-            remote(gfin.at[core, q], gfin.at[core, q], ag_s.at[0], ag_r.at[q], partner).wait_recv()
-
-        forward(q, core).start()
-        store(q, core).start()
-        return 0
-
-    lax.fori_loop(0, NQ, relay, 0)
-
-    def relayed(i, _):
-        q = turn(i)
-        forward(q, 1 - core).wait_recv()
-        store(q, 1 - core).start()
-        return 0
-
-    lax.fori_loop(0, NQ, relayed, 0)
-
-    for cp in edges + cot_pair + cot_mine + cot_its + halos + convs + [conv_pair]:
+    for cp in edges + cot_pair + cot_mine + cot_its + cot_two + halos + convs + [conv_pair]:
         cp.wait_send()
     for part in st + tt:
         for cp in part:
             cp.wait_send()
     for i in range(4):
         swap(i).wait_send()
-    for k in range(31):
-        takes, _, cp = rs_copy(k)
-
-        @pl.when(takes)
-        def _(cp=cp):
-            cp.wait_send()
 
     @pl.when(owner)
     def _():
-        for k in range(31):
-            ag_copy(k).wait_send()
-
+        few = pl.ds(0, NQ - 1)
+        remote(hb.at[few], hb.at[few], rs_s.at[0], rs_r.at[0], partner).wait_send()
+
+    @pl.when(jnp.logical_not(owner))
+    def _():
+        remote(hb, hb, rs_s.at[0], rs_r.at[0], partner).wait_send()
+
+    def forward(q, half):
+        return remote(gfin.at[half, q], gfin.at[half, q], fw_s.at[0], fw_r.at[q], partner)
+
+    def store(q, half):
+        rows = pl.ds(pl.multiple_of((half * 6 + lax.rem(q, 6)) * CH, CH), CH)
+        cols = pl.ds(pl.multiple_of(q // 6 * W, W), W)
+        pltpu.make_async_copy(gfin.at[half, q], kgrad.at[rows, cols], kg_s.at[0]).start()
+
+    def turn(i):
+        return lax.rem((x + (0, 1, 3, 2)[i // 6]) * 6 + i % 6, NQ)
+
+    lag = 4
+    for i in range(NQ + lag):
+        if i < NQ:
+            q = turn(i)
+
+            @pl.when(q != my_q)
+            def _(q=q):
+                remote(gfin.at[core, q], gfin.at[core, q], ag_s.at[0], ag_r.at[q], partner).wait_recv()
+
+            forward(q, core).start()
+            store(q, core)
+        if i >= lag:
+            q = turn(i - lag)
+            forward(q, 1 - core).wait_recv()
+            store(q, 1 - core)
+
+    @pl.when(owner)
+    def _():
+        many = rsbuf.at[pl.ds(1, 31)]
+        remote(many, many, ag_s.at[0], ag_r.at[0], partner).wait_send()
+
+    remote(gfin.at[core], gfin.at[core], fw_s.at[0], fw_r.at[0], partner).wait_send()
     for cp in outs:
         cp.wait()
-
-    def done(q, _):
-        forward(q, core).wait_send()
-        store(q, core).wait()
-        store(q, 1 - core).wait()
-        return 0
-
-    lax.fori_loop(0, NQ, done, 0)
+    pltpu.make_async_copy(kgrad, kgrad, kg_s.at[0]).wait()
 
 
 def per_device(features, gain, bias, kernel, cotangent):
@@ -483,13 +489,14 @@
             pltpu.VMEM((NZ, 1, W), F32),
             pltpu.VMEM((C, S), BF16),
             pltpu.VMEM((3, 2 * CL, S), BF16),
-            pltpu.VMEM((2, CL, S), BF16),
             pltpu.VMEM((CL, S), BF16),
+            pltpu.VMEM((CL, S), BF16),
+            pltpu.VMEM((2, CL, S), F32),
             pltpu.VMEM((2, 4, 6, CH, W), F32),
             pltpu.VMEM((4, 6, CH, W), BF16),
             pltpu.VMEM((4, 6, CH, W), BF16),
             pltpu.VMEM((NQ, CH, W), BF16),
-            pltpu.VMEM((31, CH, W), BF16),
+            pltpu.VMEM((32, CH, W), BF16),
             pltpu.VMEM((2, NQ, CH, W), BF16),
             pltpu.VMEM((9 * CL, S), F32),
             pltpu.VMEM((CL, S), F32),
@@ -502,10 +509,10 @@
             dma((14,)), dma((14,)),
             dma((4,)), dma((4,)),
             dma((4,)), dma((4,)),
-            dma((31,)), dma((31,)),
-            dma((31,)), dma((NQ,)),
-            dma((NQ,)), dma((NQ,)),
-            dma((2, NQ)),
+            dma((1,)), dma((32,)),
+            dma((1,)), dma((NQ,)),
+            dma((1,)), dma((NQ,)),
+            dma((1,)),
             dma((2,)),
         ],
         compiler_params=pltpu.CompilerParams(

time: 61.7 us -> 61.9 us (level)
  no operation moved by 1% of the time
where the time goes in v3:
time: 61.9 us; the launch traced here: 61.8 us
  Pallas kernels  58.1 us (94%)
  other arithmetic  3 us (5%)
  between operations  0.65 us (1%)
    pallas_call x1, Pallas kernels, per_device(): pl.pallas_call(body, out_shape=(jax.ShapeDtypeStruct((CL * H, W), F32), j...  58.1 us
    unnamed x1, other arithmetic  1.82 us

profile of v3, /device:TPU:1, one launch (start us, length us, event | category | flops | bytes accessed | tf_op | source)
XLA Modules:
  0.0 61.8 jit_solution(7954421337642725304)
XLA Ops:
  0.6 58.1 %strip.1 = (f32[512,128]{1,0:T(8,128)}, f32[512,128]{1,0:T(8,128)}, bf16[576,512]{1,0:T(8,128)(2,1)}) custom-call(bf16[512,128]{1,0:T(8,128)(2,1)} %bitcast.16, f32[1,64]{1,0:T(1,128)} %bitcast.18, f32[1,64]{1,0:T(1,128)} %bitcast.19, bf16[576,512]{1,0:T(8,128)(2,1)} %bitcast.15, bf16[512,128]{1,0:T(8,128)(2,1)} %bitcast.17), custom_call_target="tpu_custom_call" | custom-call | tf_op jit(solution)/shard_map/strip/pallas_call | solution.py:460
  58.8 0.0 copy-start
  58.8 1.8 %convert_bitcast_fusion = (bf16[64,1,8,128]{3,2,1,0:T(8,128)(2,1)}, bf16[64,1,8,128]{3,2,1,0:T(8,128)(2,1)}) fusion(f32[512,128]{1,0:T(8,128)} %get-tuple-element.7, f32[512,128]{1,0:T(8,128)} %get-tuple-element.6), kind=kLoop, calls=%fused_computation.1 | loop fusion | flops 131072 | bytes 786432
  60.6 0.0 copy-done
  60.6 1.2 %convert_multiply_fusion = f32[576,512]{1,0:T(8,128)} fusion(bf16[576,512]{1,0:T(8,128)(2,1)S(1)} %copy-done), kind=kLoop, calls=%fused_computation | loop fusion | flops 589824 | bytes 1769472 | tf_op jit(solution)/shard_map/mul | solution.py:533
Async XLA Ops:
  58.8 1.8 %copy-start = (bf16[576,512]{1,0:T(8,128)(2,1)S(1)}, bf16[576,512]{1,0:T(8,128)(2,1)}, u32[]{:S(2)}) copy-start(bf16[576,512]{1,0:T(8,128)(2,1)} %get-tuple-element.8) | copy-start | bytes 1769476

commit v4 on v3

--- a/solution.py
+++ b/solution.py
@@ -222,7 +222,8 @@
         pre = norm * gain_c + bias_c
         sig = jax.nn.sigmoid(pre)
         xh[:, cols] = norm
-        dact[:, cols] = sig * (1.0 + pre * (1.0 - sig)) * gain_c
+        dact[:, cols] = sig
+        x2[:, cols] = pre
         act = pre * sig
         left = jnp.where(lane == 0, rim_act[:, h:h + 1], pltpu.roll(act, 1, 1))
         right = jnp.where(lane == W - 1, rim_act[:, H + h:H + h + 1], pltpu.roll(act, W - 1, 1))
@@ -248,13 +249,14 @@
         swap(i).wait_recv()
         for rc in range(6):
             hb[lc * 6 + rc] = (g3[core, i, rc] + gcore[i, rc].astype(F32)).astype(BF16)
-        for rc in range(6):
-            q = lc * 6 + rc
-            tz = lax.rem(q, NZ)
+        for dz in (4, 3, 5, 2, 6, 1, 7, 0):
+            tz = lax.rem(z + dz, NZ)
+            rc = lax.rem(tz - lc * 6 + 4 * NZ, NZ)
+            q = lc * 6 + lax.min(rc, 5)
             ty = lax.rem(q // NZ + tz, NY)
-            slot = lax.rem(tz - z + NZ, NZ) * NY + lax.rem(ty - yh + NY, NY)
-
-            @pl.when(q != my_q)
+            slot = dz * NY + lax.rem(ty - yh + NY, NY)
+
+            @pl.when((rc < 6) & (q != my_q))
             def _(q=q, tz=tz, ty=ty, slot=slot):
                 remote(hb.at[q], rsbuf.at[slot], rs_s.at[0], rs_r.at[slot], to(tz, ty)).start()
 
@@ -332,7 +334,8 @@
         agrad = agrad + jnp.where(lane == W - 1, rim0[:, H + h:H + h + 1], pltpu.roll(u[0], W - 1, 1))
         agrad = agrad + jnp.where(lane == 0, rim2[:, h:h + 1], pltpu.roll(u[2], 1, 1))
         cols = slice(h * W, (h + 1) * W)
-        ng = agrad * dact[:, cols]
+        sig = dact[:, cols]
+        ng = agrad * sig * (1.0 + x2[:, cols] * (1.0 - sig)) * gain_c
         agr[:, cols] = ng
         t1 += ng
         t2 += ng * xh[:, cols]
@@ -340,10 +343,14 @@
     tt = rounds((z_t, c_t, y_t), t_s, t_r)
     start(tt[0])
 
+    def chunk(half, q):
+        rows = pl.ds(pl.multiple_of(lax.rem(q, 6) * CH, CH), CH)
+        return gfin.at[half, q // 6, rows]
+
     def ag_copy(dz, dy):
         q = lax.min(my_j, 2) * NZ + z
         dev = to(lax.rem(z + dz, NZ), lax.rem(yh + dy, NY))
-        return remote(gfin.at[core, q], gfin.at[core, q], ag_s.at[0], ag_r.at[q], dev)
+        return remote(chunk(core, q), chunk(core, q), ag_s.at[0], ag_r.at[q], dev)
 
     @pl.when(owner)
     def _():
@@ -352,16 +359,13 @@
             slot = dz * NY + dy
             remote(hb.at[0], rsbuf.at[slot], rs_s.at[0], rs_r.at[slot], partner).wait_recv()
             acc = acc + rsbuf[slot].astype(F32)
-        gfin[core, my_q] = acc.astype(BF16)
+        gfin[core, my_q // 6, pl.ds(pl.multiple_of(lax.rem(my_q, 6) * CH, CH), CH)] = acc.astype(BF16)
         for dz, dy in reversed(NEAR):
             ag_copy(dz, dy).start()
 
     arrive(tt[0])
     c_t[0] = add_up(z_t)
     start(tt[1])
-    arrive(tt[1])
-    y_t[0] = add_up(c_t)
-    start(tt[2])
 
     arrive(convs)
 
@@ -377,7 +381,56 @@
         convp[:, h * W:(h + 1) * W] = pair_sum(1 - yl, h).astype(BF16)
     conv_pair = remote(convp, convq, conv_s.at[0], conv_r.at[0], beside)
     conv_pair.start()
-
+    arrive(tt[1])
+    y_t[0] = add_up(c_t)
+    start(tt[2])
+
+    for cp in edges + cot_pair + cot_mine + cot_its + cot_two + halos + convs:
+        cp.wait_send()
+    for part in st + tt[:2]:
+        for cp in part:
+            cp.wait_send()
+    for i in range(4):
+        swap(i).wait_send()
+
+    @pl.when(owner)
+    def _():
+        few = pl.ds(0, NQ - 1)
+        remote(hb.at[few], hb.at[few], rs_s.at[0], rs_r.at[0], partner).wait_send()
+
+    @pl.when(jnp.logical_not(owner))
+    def _():
+        remote(hb, hb, rs_s.at[0], rs_r.at[0], partner).wait_send()
+
+    def forward(i, half):
+        lc = lax.rem(x + (0, 1, 3, 2)[i], 4)
+        return remote(gfin.at[half, lc], gfin.at[half, lc], fw_s.at[i], fw_r.at[i], partner)
+
+    def store(i, half):
+        lc = lax.rem(x + (0, 1, 3, 2)[i], 4)
+        rows = pl.ds(pl.multiple_of(half * 6 * CH, 6 * CH), 6 * CH)
+        cols = pl.ds(pl.multiple_of(lc * W, W), W)
+        return pltpu.make_async_copy(gfin.at[half, lc], kgrad.at[rows, cols], kg_s.at[half, i])
+
+    def relay(i):
+        lc = lax.rem(x + (0, 1, 3, 2)[i], 4)
+        for rc in range(6):
+            q = lc * 6 + rc
+
+            @pl.when(q != my_q)
+            def _(q=q):
+                remote(chunk(core, q), chunk(core, q), ag_s.at[0], ag_r.at[q], partner).wait_recv()
+
+        forward(i, core).start()
+        store(i, core).start()
+
+    def relayed(i):
+        forward(i, 1 - core).wait_recv()
+        store(i, 1 - core).start()
+
+    relay(0)
+    relay(1)
+    relay(2)
     arrive(tt[2])
     q1, q2 = unpack(add_up(y_t))
     q1 = q1 / n
@@ -398,59 +451,51 @@
         conv_f[pl.ds(h, CL, stride=H), :] = pair_sum(yl, h) + convq[:, cols].astype(F32)
     outs[1].start()
 
-    for cp in edges + cot_pair + cot_mine + cot_its + cot_two + halos + convs + [conv_pair]:
-        cp.wait_send()
-    for part in st + tt:
-        for cp in part:
-            cp.wait_send()
-    for i in range(4):
-        swap(i).wait_send()
-
-    @pl.when(owner)
-    def _():
-        few = pl.ds(0, NQ - 1)
-        remote(hb.at[few], hb.at[few], rs_s.at[0], rs_r.at[0], partner).wait_send()
-
-    @pl.when(jnp.logical_not(owner))
-    def _():
-        remote(hb, hb, rs_s.at[0], rs_r.at[0], partner).wait_send()
-
-    def forward(q, half):
-        return remote(gfin.at[half, q], gfin.at[half, q], fw_s.at[0], fw_r.at[q], partner)
-
-    def store(q, half):
-        rows = pl.ds(pl.multiple_of((half * 6 + lax.rem(q, 6)) * CH, CH), CH)
-        cols = pl.ds(pl.multiple_of(q // 6 * W, W), W)
-        pltpu.make_async_copy(gfin.at[half, q], kgrad.at[rows, cols], kg_s.at[0]).start()
-
-    def turn(i):
-        return lax.rem((x + (0, 1, 3, 2)[i // 6]) * 6 + i % 6, NQ)
-
-    lag = 4
-    for i in range(NQ + lag):
-        if i < NQ:
-            q = turn(i)
-
-            @pl.when(q != my_q)
-            def _(q=q):
-                remote(gfin.at[core, q], gfin.at[core, q], ag_s.at[0], ag_r.at[q], partner).wait_recv()
-
-            forward(q, core).start()
-            store(q, core)
-        if i >= lag:
-            q = turn(i - lag)
-            forward(q, 1 - core).wait_recv()
-            store(q, 1 - core)
+    relayed(0)
+    relayed(1)
+    relayed(2)
+    relay(3)
 
     @pl.when(owner)
     def _():
         many = rsbuf.at[pl.ds(1, 31)]
         remote(many, many, ag_s.at[0], ag_r.at[0], partner).wait_send()
 
-    remote(gfin.at[core], gfin.at[core], fw_s.at[0], fw_r.at[0], partner).wait_send()
+    for cp in tt[2] + [conv_pair]:
+        cp.wait_send()
+    for i in range(3):
+        forward(i, core).wait_send()
+    relayed(3)
+    forward(3, core).wait_send()
     for cp in outs:
         cp.wait()
-    pltpu.make_async_copy(kgrad, kgrad, kg_s.at[0]).wait()
+    for i in range(4):
+        store(i, core).wait()
+        store(i, 1 - core).wait()
+
+
+def finish(conv_in, fg_in, kg_in, conv_out, fg_out, kg_out, conv_a, fg_a, kg_a, conv_b, fg_b, kg_b, sem):
+    loads = [
+        pltpu.make_async_copy(a, b, sem.at[i])
+        for i, (a, b) in enumerate(((conv_in, conv_a), (fg_in, fg_a), (kg_in, kg_a)))
+    ]
+    stores = [
+        pltpu.make_async_copy(a, b, sem.at[3 + i])
+        for i, (a, b) in enumerate(((conv_b, conv_out), (fg_b, fg_out), (kg_b, kg_out)))
+    ]
+    for i in (2, 0, 1):
+        loads[i].start()
+    loads[2].wait()
+    kg_b[...] = kg_a[...].astype(F32) * (2.0 ** -8)
+    stores[2].start()
+    loads[0].wait()
+    conv_b[...] = conv_a[...].astype(BF16)
+    stores[0].start()
+    loads[1].wait()
+    fg_b[...] = fg_a[...].astype(BF16)
+    stores[1].start()
+    for cp in stores:
+        cp.wait()
 
 
 def per_device(features, gain, bias, kernel, cotangent):
@@ -497,7 +542,7 @@
             pltpu.VMEM((4, 6, CH, W), BF16),
             pltpu.VMEM((NQ, CH, W), BF16),
             pltpu.VMEM((32, CH, W), BF16),
-            pltpu.VMEM((2, NQ, CH, W), BF16),
+            pltpu.VMEM((2, 4, 6 * CH, W), BF16),
             pltpu.VMEM((9 * CL, S), F32),
             pltpu.VMEM((CL, S), F32),
             pltpu.VMEM((CL * H, W), F32),
@@ -511,8 +556,8 @@
             dma((4,)), dma((4,)),
             dma((1,)), dma((32,)),
             dma((1,)), dma((NQ,)),
-            dma((1,)), dma((NQ,)),
-            dma((1,)),
+            dma((4,)), dma((4,)),
+            dma((2, 4)),
             dma((2,)),
         ],
         compiler_params=pltpu.CompilerParams(
@@ -526,11 +571,22 @@
         kernel.reshape(9 * CL, C),
         cotangent.reshape(CL * H, W),
     )
+    maps = ((CL * H, W), F32), ((CL * H, W), F32), ((9 * CL, C), BF16)
+    ends = ((CL * H, W), BF16), ((CL * H, W), BF16), ((9 * CL, C), F32)
+    conv_out, fgrad, kgrad = pl.pallas_call(
+        finish,
+        out_shape=tuple(jax.ShapeDtypeStruct(*a) for a in ends),
+        in_specs=[hbm] * 3,
+        out_specs=(hbm,) * 3,
+        scratch_shapes=[pltpu.VMEM(*a) for a in maps + ends] + [dma((6,))],
+        compiler_params=pltpu.CompilerParams(vmem_limit_bytes=62 * 1024 * 1024),
+        name="finish",
+    )(conv_out, fgrad, kgrad)
     shape = features.shape
     return (
-        conv_out.astype(BF16).reshape(shape),
-        fgrad.astype(BF16).reshape(shape),
-        (kgrad.astype(F32) * (2.0 ** -8)).reshape(kernel.shape),
+        conv_out.reshape(shape),
+        fgrad.reshape(shape),
+        kgrad.reshape(kernel.shape),
     )
 
 

time: 61.9 us -> 60 us (0.969); the launches traced: 61.8 us -> 58.9 us
  other arithmetic: 3 us -> 0 us
    pallas_call x0 -> x1, Pallas kernels: none -> 2.28 us  [per_device(): pl.pallas_call(finish, out_shape=tuple((jax.ShapeDtypeStruct(*a) for a in...]
    pallas_call x1, Pallas kernels: 58.1 us -> 56 us  [per_device(): pl.pallas_call(body, out_shape=(jax.ShapeDtypeStruct((CL * H, W), F32), j...]
    unnamed x1 -> x0, other arithmetic: 1.82 us -> none
    mul x1 -> x0, other arithmetic: 1.17 us -> none  [per_device(): kgrad.astype(F32) * 2.0 ** (-8)]
where the time goes in v4:
time: 60 us; the launch traced here: 58.9 us
  Pallas kernels  58.3 us (97%)
  between operations  0.64 us (1%)
    pallas_call x1, Pallas kernels, per_device(): pl.pallas_call(body, out_shape=(jax.ShapeDtypeStruct((CL * H, W), F32), j...  56 us
    pallas_call x1, Pallas kernels, per_device(): pl.pallas_call(finish, out_shape=tuple((jax.ShapeDtypeStruct(*a) for a in...  2.28 us

profile of v4, /device:TPU:1, one launch (start us, length us, event | category | flops | bytes accessed | tf_op | source)
XLA Modules:
  0.0 58.9 jit_solution(9639506722417525550)
XLA Ops:
  0.6 56.0 %strip.1 = (f32[512,128]{1,0:T(8,128)}, f32[512,128]{1,0:T(8,128)}, bf16[576,512]{1,0:T(8,128)(2,1)}) custom-call(bf16[512,128]{1,0:T(8,128)(2,1)} %bitcast.13, f32[1,64]{1,0:T(1,128)} %bitcast.15, f32[1,64]{1,0:T(1,128)} %bitcast.16, bf16[576,512]{1,0:T(8,128)(2,1)} %bitcast.12, bf16[512,128]{1,0:T(8,128)(2,1)} %bitcast.14), custom_call_target="tpu_custom_call" | custom-call | tf_op jit(solution)/shard_map/strip/pallas_call | solution.py:505
  56.7 2.3 %finish.1 = (bf16[512,128]{1,0:T(8,128)(2,1)}, bf16[512,128]{1,0:T(8,128)(2,1)}, f32[576,512]{1,0:T(8,128)}) custom-call(f32[512,128]{1,0:T(8,128)} %get-tuple-element.9.conv_in, f32[512,128]{1,0:T(8,128)} %get-tuple-element.10.fg_in, bf16[576,512]{1,0:T(8,128)(2,1)} %get-tuple-element.11.kg_in), custom_call_target="tpu_custom_call" | custom-call | tf_op jit(solution)/shard_map/finish/pallas_call | solution.py:576

commit v5 on v4

--- a/solution.py
+++ b/solution.py
@@ -26,9 +26,9 @@
 
 
 def body(
-    feat_in, gain, bias, w_in, cot_in,
+    feat_in, gain_in, bias_in, w_in, cot_in,
     conv_out, fgrad, kgrad,
-    feat, cot, w, in_s, tmp, x2, xh, dact, patch, wt, cotall, halo, edge, edge_in,
+    feat, cot, w, gain, bias, in_s, tmp, x2, xh, dact, patch, wt, cotall, halo, edge, edge_in,
     c_st, y_st, z_st, c_t, y_t, z_t,
     convb, convr, convp, convq, convown, g3, gsend, gcore, hb, rsbuf, gfin, zz, agr, conv_f, fg_f,
     edge_s, edge_r, cot_s, cot_r, halo_s, halo_r, st_s, st_r, t_s, t_r,
@@ -66,7 +66,9 @@
 
     loads = [
         pltpu.make_async_copy(a, b, in_s.at[i])
-        for i, (a, b) in enumerate(((feat_in, feat), (cot_in, cot), (w_in, w)))
+        for i, (a, b) in enumerate((
+            (feat_in, feat), (cot_in, cot), (w_in, w), (gain_in, gain), (bias_in, bias)
+        ))
     ]
     for cp in loads:
         cp.start()
@@ -201,6 +203,8 @@
     ]
     start(halos)
 
+    loads[3].wait()
+    loads[4].wait()
     gain_c = column(gain)
     bias_c = column(bias)
     n = float(16 * H * W * n_lon)
@@ -234,7 +238,7 @@
                 if 0 <= to < H:
                     patch[r * 192 + s * CL:r * 192 + (s + 1) * CL, to * W:(to + 1) * W] = v
 
-    my_j = lax.rem(yh - z + 8, 4)
+    my_j = lax.rem(yh - z + 2 * core + 8, 4)
     my_q = my_j * NZ + z
     owner = my_j < 3
 
@@ -253,7 +257,7 @@
             tz = lax.rem(z + dz, NZ)
             rc = lax.rem(tz - lc * 6 + 4 * NZ, NZ)
             q = lc * 6 + lax.min(rc, 5)
-            ty = lax.rem(q // NZ + tz, NY)
+            ty = lax.rem(q // NZ + tz + 2 * core, NY)
             slot = dz * NY + lax.rem(ty - yh + NY, NY)
 
             @pl.when((rc < 6) & (q != my_q))
@@ -380,7 +384,6 @@
     for h in range(H):
         convp[:, h * W:(h + 1) * W] = pair_sum(1 - yl, h).astype(BF16)
     conv_pair = remote(convp, convq, conv_s.at[0], conv_r.at[0], beside)
-    conv_pair.start()
     arrive(tt[1])
     y_t[0] = add_up(c_t)
     start(tt[2])
@@ -429,6 +432,7 @@
         store(i, 1 - core).start()
 
     relay(0)
+    conv_pair.start()
     relay(1)
     relay(2)
     arrive(tt[2])
@@ -445,6 +449,7 @@
     ]
     outs[0].start()
 
+    relay(3)
     arrive([conv_pair])
     for h in range(H):
         cols = slice(h * W, (h + 1) * W)
@@ -454,7 +459,6 @@
     relayed(0)
     relayed(1)
     relayed(2)
-    relay(3)
 
     @pl.when(owner)
     def _():
@@ -475,31 +479,34 @@
 
 
 def finish(conv_in, fg_in, kg_in, conv_out, fg_out, kg_out, conv_a, fg_a, kg_a, conv_b, fg_b, kg_b, sem):
+    pieces = [pl.ds(i * 144, 144) for i in range(4)]
+    kg_loads = [pltpu.make_async_copy(kg_in.at[p], kg_a.at[p], sem.at[i]) for i, p in enumerate(pieces)]
+    kg_stores = [pltpu.make_async_copy(kg_b.at[p], kg_out.at[p], sem.at[4 + i]) for i, p in enumerate(pieces)]
     loads = [
-        pltpu.make_async_copy(a, b, sem.at[i])
-        for i, (a, b) in enumerate(((conv_in, conv_a), (fg_in, fg_a), (kg_in, kg_a)))
+        pltpu.make_async_copy(conv_in, conv_a, sem.at[8]),
+        pltpu.make_async_copy(fg_in, fg_a, sem.at[9]),
     ]
     stores = [
-        pltpu.make_async_copy(a, b, sem.at[3 + i])
-        for i, (a, b) in enumerate(((conv_b, conv_out), (fg_b, fg_out), (kg_b, kg_out)))
-    ]
-    for i in (2, 0, 1):
-        loads[i].start()
-    loads[2].wait()
-    kg_b[...] = kg_a[...].astype(F32) * (2.0 ** -8)
-    stores[2].start()
+        pltpu.make_async_copy(conv_b, conv_out, sem.at[10]),
+        pltpu.make_async_copy(fg_b, fg_out, sem.at[11]),
+    ]
+    for cp in kg_loads + loads:
+        cp.start()
+    for i, p in enumerate(pieces):
+        kg_loads[i].wait()
+        kg_b[p, :] = kg_a[p, :].astype(F32) * (2.0 ** -8)
+        kg_stores[i].start()
     loads[0].wait()
     conv_b[...] = conv_a[...].astype(BF16)
     stores[0].start()
     loads[1].wait()
     fg_b[...] = fg_a[...].astype(BF16)
     stores[1].start()
-    for cp in stores:
+    for cp in kg_stores + stores:
         cp.wait()
 
 
 def per_device(features, gain, bias, kernel, cotangent):
-    vmem = pl.BlockSpec(memory_space=pltpu.VMEM)
     hbm = pl.BlockSpec(memory_space=pltpu.HBM)
     dma = pltpu.SemaphoreType.DMA
     conv_out, fgrad, kgrad = pl.pallas_call(
@@ -509,13 +516,15 @@
             jax.ShapeDtypeStruct((CL * H, W), F32),
             jax.ShapeDtypeStruct((9 * CL, C), BF16),
         ),
-        in_specs=[hbm, vmem, vmem, hbm, hbm],
+        in_specs=[hbm] * 5,
         out_specs=(hbm,) * 3,
         scratch_shapes=[
             pltpu.VMEM((CL * H, W), BF16),
             pltpu.VMEM((CL * H, W), BF16),
             pltpu.VMEM((9 * CL, C), BF16),
-            dma((3,)),
+            pltpu.VMEM((1, CL), F32),
+            pltpu.VMEM((1, CL), F32),
+            dma((5,)),
             pltpu.VMEM((CL * H, W), F32),
             pltpu.VMEM((CL, S), F32),
             pltpu.VMEM((CL, S), F32),
@@ -578,7 +587,7 @@
         out_shape=tuple(jax.ShapeDtypeStruct(*a) for a in ends),
         in_specs=[hbm] * 3,
         out_specs=(hbm,) * 3,
-        scratch_shapes=[pltpu.VMEM(*a) for a in maps + ends] + [dma((6,))],
+        scratch_shapes=[pltpu.VMEM(*a) for a in maps + ends] + [dma((12,))],
         compiler_params=pltpu.CompilerParams(vmem_limit_bytes=62 * 1024 * 1024),
         name="finish",
     )(conv_out, fgrad, kgrad)

time: 60 us -> 55.7 us (0.928); the launches traced: 58.9 us -> 55.6 us
  Pallas kernels: 58.3 us -> 54.9 us
    pallas_call x1, Pallas kernels: 56 us -> 52.8 us  [per_device(): pl.pallas_call(body, out_shape=(jax.ShapeDtypeStruct((CL * H, W), F32), j...]
where the time goes in v5:
time: 55.7 us; the launch traced here: 55.6 us
  Pallas kernels  54.9 us (99%)
  between operations  0.64 us (1%)
    pallas_call x1, Pallas kernels, per_device(): pl.pallas_call(body, out_shape=(jax.ShapeDtypeStruct((CL * H, W), F32), j...  52.8 us
    pallas_call x1, Pallas kernels, per_device(): pl.pallas_call(finish, out_shape=tuple((jax.ShapeDtypeStruct(*a) for a in...  2.12 us

profile of v5, /device:TPU:1, one launch (start us, length us, event | category | flops | bytes accessed | tf_op | source)
XLA Modules:
  0.0 55.6 jit_solution(13032166821236259798)
XLA Ops:
  0.6 52.8 %strip.1 = (f32[512,128]{1,0:T(8,128)}, f32[512,128]{1,0:T(8,128)}, bf16[576,512]{1,0:T(8,128)(2,1)}) custom-call(bf16[512,128]{1,0:T(8,128)(2,1)} %bitcast.13, f32[1,64]{1,0:T(1,128)} %bitcast.15, f32[1,64]{1,0:T(1,128)} %bitcast.16, bf16[576,512]{1,0:T(8,128)(2,1)} %bitcast.12, bf16[512,128]{1,0:T(8,128)(2,1)} %bitcast.14), custom_call_target="tpu_custom_call" | custom-call | tf_op jit(solution)/shard_map/strip/pallas_call | solution.py:512
  53.5 2.1 %finish.1 = (bf16[512,128]{1,0:T(8,128)(2,1)}, bf16[512,128]{1,0:T(8,128)(2,1)}, f32[576,512]{1,0:T(8,128)}) custom-call(f32[512,128]{1,0:T(8,128)} %get-tuple-element.9.conv_in, f32[512,128]{1,0:T(8,128)} %get-tuple-element.10.fg_in, bf16[576,512]{1,0:T(8,128)(2,1)} %get-tuple-element.11.kg_in), custom_call_target="tpu_custom_call" | custom-call | tf_op jit(solution)/shard_map/finish/pallas_call | solution.py:585

commit v6 on v5

--- a/solution.py
+++ b/solution.py
@@ -435,6 +435,7 @@
     conv_pair.start()
     relay(1)
     relay(2)
+    relay(3)
     arrive(tt[2])
     q1, q2 = unpack(add_up(y_t))
     q1 = q1 / n
@@ -449,7 +450,6 @@
     ]
     outs[0].start()
 
-    relay(3)
     arrive([conv_pair])
     for h in range(H):
         cols = slice(h * W, (h + 1) * W)

time: 55.7 us -> 54.5 us (0.978)
  Pallas kernels: 54.9 us -> 53.5 us
    pallas_call x1, Pallas kernels: 52.8 us -> 51.4 us  [per_device(): pl.pallas_call(body, out_shape=(jax.ShapeDtypeStruct((CL * H, W), F32), j...]
where the time goes in v6:
time: 54.5 us; the launch traced here: 54.2 us
  Pallas kernels  53.5 us (98%)
  between operations  0.64 us (1%)
    pallas_call x1, Pallas kernels, per_device(): pl.pallas_call(body, out_shape=(jax.ShapeDtypeStruct((CL * H, W), F32), j...  51.4 us
    pallas_call x1, Pallas kernels, per_device(): pl.pallas_call(finish, out_shape=tuple((jax.ShapeDtypeStruct(*a) for a in...  2.12 us

profile of v6, /device:TPU:1, one launch (start us, length us, event | category | flops | bytes accessed | tf_op | source)
XLA Modules:
  0.0 54.2 jit_solution(15494985640672461902)
XLA Ops:
  0.6 51.4 %strip.1 = (f32[512,128]{1,0:T(8,128)}, f32[512,128]{1,0:T(8,128)}, bf16[576,512]{1,0:T(8,128)(2,1)}) custom-call(bf16[512,128]{1,0:T(8,128)(2,1)} %bitcast.13, f32[1,64]{1,0:T(1,128)} %bitcast.15, f32[1,64]{1,0:T(1,128)} %bitcast.16, bf16[576,512]{1,0:T(8,128)(2,1)} %bitcast.12, bf16[512,128]{1,0:T(8,128)(2,1)} %bitcast.14), custom_call_target="tpu_custom_call" | custom-call | tf_op jit(solution)/shard_map/strip/pallas_call | solution.py:512
  52.0 2.1 %finish.1 = (bf16[512,128]{1,0:T(8,128)(2,1)}, bf16[512,128]{1,0:T(8,128)(2,1)}, f32[576,512]{1,0:T(8,128)}) custom-call(f32[512,128]{1,0:T(8,128)} %get-tuple-element.9.conv_in, f32[512,128]{1,0:T(8,128)} %get-tuple-element.10.fg_in, bf16[576,512]{1,0:T(8,128)(2,1)} %get-tuple-element.11.kg_in), custom_call_target="tpu_custom_call" | custom-call | tf_op jit(solution)/shard_map/finish/pallas_call | solution.py:585

commit v7 on v6

--- a/solution.py
+++ b/solution.py
@@ -177,11 +177,6 @@
         remote(edge, edge_in.at[1], edge_s.at[1], edge_r.at[1], at_lon(-1)),
     ]
     start(edges)
-    loads[2].wait()
-    for i in range(4):
-        wt[:, i * 128:(i + 1) * 128] = w[i * 128:(i + 1) * 128, :].astype(F32).T.astype(BF16)
-    wt[:, 512:576] = w[512:576, :].astype(F32).T.astype(BF16)
-
     arrive(cot_pair)
     start(cot_its)
     arrive(st[0])
@@ -202,6 +197,11 @@
         for k in range(1, 8)
     ]
     start(halos)
+
+    loads[2].wait()
+    for i in range(4):
+        wt[:, i * 128:(i + 1) * 128] = w[i * 128:(i + 1) * 128, :].astype(F32).T.astype(BF16)
+    wt[:, 512:576] = w[512:576, :].astype(F32).T.astype(BF16)
 
     loads[3].wait()
     loads[4].wait()
@@ -371,6 +371,54 @@
     c_t[0] = add_up(z_t)
     start(tt[1])
 
+    arrive(tt[1])
+    y_t[0] = add_up(c_t)
+    start(tt[2])
+
+    for cp in edges + cot_pair + cot_mine + cot_its + cot_two + halos:
+        cp.wait_send()
+    for part in st + tt[:2]:
+        for cp in part:
+            cp.wait_send()
+    for i in range(4):
+        swap(i).wait_send()
+
+    @pl.when(owner)
+    def _():
+        few = pl.ds(0, NQ - 1)
+        remote(hb.at[few], hb.at[few], rs_s.at[0], rs_r.at[0], partner).wait_send()
+
+    @pl.when(jnp.logical_not(owner))
+    def _():
+        remote(hb, hb, rs_s.at[0], rs_r.at[0], partner).wait_send()
+
+    def forward(i, half):
+        lc = lax.rem(x + (0, 1, 3, 2)[i], 4)
+        return remote(gfin.at[half, lc], gfin.at[half, lc], fw_s.at[i], fw_r.at[i], partner)
+
+    def store(i, half):
+        lc = lax.rem(x + (0, 1, 3, 2)[i], 4)
+        rows = pl.ds(pl.multiple_of(half * 6 * CH, 6 * CH), 6 * CH)
+        cols = pl.ds(pl.multiple_of(lc * W, W), W)
+        return pltpu.make_async_copy(gfin.at[half, lc], kgrad.at[rows, cols], kg_s.at[half, i])
+
+    def relay(i):
+        lc = lax.rem(x + (0, 1, 3, 2)[i], 4)
+        for rc in range(6):
+            q = lc * 6 + rc
+
+            @pl.when(q != my_q)
+            def _(q=q):
+                remote(chunk(core, q), chunk(core, q), ag_s.at[0], ag_r.at[q], partner).wait_recv()
+
+        forward(i, core).start()
+        store(i, core).start()
+
+    def relayed(i):
+        forward(i, 1 - core).wait_recv()
+        store(i, 1 - core).start()
+
+    relay(0)
     arrive(convs)
 
     def pair_sum(half, h):
@@ -384,54 +432,6 @@
     for h in range(H):
         convp[:, h * W:(h + 1) * W] = pair_sum(1 - yl, h).astype(BF16)
     conv_pair = remote(convp, convq, conv_s.at[0], conv_r.at[0], beside)
-    arrive(tt[1])
-    y_t[0] = add_up(c_t)
-    start(tt[2])
-
-    for cp in edges + cot_pair + cot_mine + cot_its + cot_two + halos + convs:
-        cp.wait_send()
-    for part in st + tt[:2]:
-        for cp in part:
-            cp.wait_send()
-    for i in range(4):
-        swap(i).wait_send()
-
-    @pl.when(owner)
-    def _():
-        few = pl.ds(0, NQ - 1)
-        remote(hb.at[few], hb.at[few], rs_s.at[0], rs_r.at[0], partner).wait_send()
-
-    @pl.when(jnp.logical_not(owner))
-    def _():
-        remote(hb, hb, rs_s.at[0], rs_r.at[0], partner).wait_send()
-
-    def forward(i, half):
-        lc = lax.rem(x + (0, 1, 3, 2)[i], 4)
-        return remote(gfin.at[half, lc], gfin.at[half, lc], fw_s.at[i], fw_r.at[i], partner)
-
-    def store(i, half):
-        lc = lax.rem(x + (0, 1, 3, 2)[i], 4)
-        rows = pl.ds(pl.multiple_of(half * 6 * CH, 6 * CH), 6 * CH)
-        cols = pl.ds(pl.multiple_of(lc * W, W), W)
-        return pltpu.make_async_copy(gfin.at[half, lc], kgrad.at[rows, cols], kg_s.at[half, i])
-
-    def relay(i):
-        lc = lax.rem(x + (0, 1, 3, 2)[i], 4)
-        for rc in range(6):
-            q = lc * 6 + rc
-
-            @pl.when(q != my_q)
-            def _(q=q):
-                remote(chunk(core, q), chunk(core, q), ag_s.at[0], ag_r.at[q], partner).wait_recv()
-
-        forward(i, core).start()
-        store(i, core).start()
-
-    def relayed(i):
-        forward(i, 1 - core).wait_recv()
-        store(i, 1 - core).start()
-
-    relay(0)
     conv_pair.start()
     relay(1)
     relay(2)
@@ -465,7 +465,7 @@
         many = rsbuf.at[pl.ds(1, 31)]
         remote(many, many, ag_s.at[0], ag_r.at[0], partner).wait_send()
 
-    for cp in tt[2] + [conv_pair]:
+    for cp in tt[2] + convs + [conv_pair]:
         cp.wait_send()
     for i in range(3):
         forward(i, core).wait_send()

time: 54.5 us -> 54.6 us (level)
  no operation moved by 1% of the time
where the time goes in v7:
time: 54.6 us; the launch traced here: 54 us
  Pallas kernels  53.4 us (98%)
  between operations  0.64 us (1%)
    pallas_call x1, Pallas kernels, per_device(): pl.pallas_call(body, out_shape=(jax.ShapeDtypeStruct((CL * H, W), F32), j...  51.2 us
    pallas_call x1, Pallas kernels, per_device(): pl.pallas_call(finish, out_shape=tuple((jax.ShapeDtypeStruct(*a) for a in...  2.12 us

profile of v7, /device:TPU:1, one launch (start us, length us, event | category | flops | bytes accessed | tf_op | source)
XLA Modules:
  0.0 54.0 jit_solution(1336445288267008779)
XLA Ops:
  0.6 51.2 %strip.1 = (f32[512,128]{1,0:T(8,128)}, f32[512,128]{1,0:T(8,128)}, bf16[576,512]{1,0:T(8,128)(2,1)}) custom-call(bf16[512,128]{1,0:T(8,128)(2,1)} %bitcast.13, f32[1,64]{1,0:T(1,128)} %bitcast.15, f32[1,64]{1,0:T(1,128)} %bitcast.16, bf16[576,512]{1,0:T(8,128)(2,1)} %bitcast.12, bf16[512,128]{1,0:T(8,128)(2,1)} %bitcast.14), custom_call_target="tpu_custom_call" | custom-call | tf_op jit(solution)/shard_map/strip/pallas_call | solution.py:512
  51.9 2.1 %finish.1 = (bf16[512,128]{1,0:T(8,128)(2,1)}, bf16[512,128]{1,0:T(8,128)(2,1)}, f32[576,512]{1,0:T(8,128)}) custom-call(f32[512,128]{1,0:T(8,128)} %get-tuple-element.9.conv_in, f32[512,128]{1,0:T(8,128)} %get-tuple-element.10.fg_in, bf16[576,512]{1,0:T(8,128)(2,1)} %get-tuple-element.11.kg_in), custom_call_target="tpu_custom_call" | custom-call | tf_op jit(solution)/shard_map/finish/pallas_call | solution.py:585
